TPU v7x, 128 devices: a whole 4x4x4 slice. The times are simulated.
128 devices in a mesh: slab: 32 (over x, z, core), blk: 4 (over y).
Axes of the slice: x: 4, y: 4, z: 4, core: 2. Of those that a mesh axis runs over, the one named last changes fastest.
Arguments:
- thermal_level: float32 [512, 64, 256], P('slab', 'blk'), may hold values from -6 to 6
- deformation_vector: float32 [3, 512, 64, 256], P(None, 'slab', 'blk'), may hold values from -6 to 6
- thermal_elastic_modulus: float32 [512, 64, 256], P('slab', 'blk'), may hold values from 0.25 to 1
- yield_strain: float32 [512, 64, 256], P('slab', 'blk'), may hold values from 0.05 to 2
- refinement_flag: int32 [32, 4, 16], P('slab', 'blk'), may hold values 0 or 1
- destination_holder: int32 [32, 4, 16], P('slab', 'blk'), may hold values from 0 to 31, as said below
- destination_position: int32 [32, 4, 16], P('slab', 'blk'), may hold values from 0 to 15, as said below
Outputs:
- relaxed_thermal_entries: float32 [32, 4, 16, 4096], P('slab', 'blk')
- relaxed_deformation_entries: float32 [32, 4, 16, 3, 4096], P('slab', 'blk')
- redistributed_yield_strain: float32 [32, 4, 16, 4096], P('slab', 'blk')
Inputs may be any that keep to these rules, and one draw needn't show every extreme that they name: For each blk index b there is an ordering r of the slab indices and a step t_p for each slot p such that destination_holder[s,b,p] = r[(position of s in r + t_p) mod the number of slab indices]; no step is taken by more than 2 slots and one step by exactly 2, so one device hands at most 2 patches to one device and reaches 2. For each blk index, (destination_holder, destination_position) maps the patches one to one onto slab indices times slots: every device receives exactly 16 patches.
All inputs are finite; a program needn't handle non-finite values. No bound on the sum of `refinement_flag` on one device may be relied on, other than what follows from the above.
Results may differ from a plain program's by a relative error of at most 0.0003.
Values may be sent and summed in bfloat16 or wider, within the bound.
A program may use at most 192 MiB of HBM per device.

v0:
```python
import jax
import jax.numpy as jnp
from jax import lax
from jax.sharding import PartitionSpec as P

EDGE = 16
SWEEPS = 4
SMOOTH = 2


time_step = 0.12
coupling = 1.0


def extended(block, sides, width):
    for axis, dim in sides:
        count = lax.axis_size(axis)
        forward = [(i, i + 1) for i in range(count - 1)]
        backward = [(target, source) for source, target in forward]
        low = lax.ppermute(
            lax.slice_in_dim(block, block.shape[dim] - width, None, axis=dim), axis, forward
        )
        high = lax.ppermute(lax.slice_in_dim(block, 0, width, axis=dim), axis, backward)
        block = jnp.concatenate([low, block, high], axis=dim)
    return block


def face_list():
    return [(1, 0, 0), (-1, 0, 0), (0, 1, 0), (0, -1, 0), (0, 0, 1), (0, 0, -1)]


def tile_directions():
    result = []
    for shift_x in (-1, 0, 1):
        for shift_y in (-1, 0, 1):
            for shift_z in (-1, 0, 1):
                reach = abs(shift_x) + abs(shift_y) + abs(shift_z)
                if reach > 0:
                    result.append((shift_x, shift_y, shift_z, [0.0, 0.1, 0.04, 0.02][reach]))
    return result


def window(padded, shift_x, shift_y, shift_z):
    size_x, size_y, size_z = padded.shape[-3:]
    return padded[
        ...,
        1 + shift_x : size_x - 1 + shift_x,
        1 + shift_y : size_y - 1 + shift_y,
        1 + shift_z : size_z - 1 + shift_z,
    ]


def sweep_core(heat_pad, moved_pad, conduct_pad):
    centre_heat = window(heat_pad, 0, 0, 0)
    centre_moved = window(moved_pad, 0, 0, 0)
    centre_conduct = window(conduct_pad, 0, 0, 0)
    flux = jnp.zeros_like(centre_heat)
    laplace = jnp.zeros_like(centre_moved)
    for shift_x, shift_y, shift_z in face_list():
        flux = flux + 0.5 * (centre_conduct + window(conduct_pad, shift_x, shift_y, shift_z)) * (
            window(heat_pad, shift_x, shift_y, shift_z) - centre_heat
        )
        laplace = laplace + window(moved_pad, shift_x, shift_y, shift_z) - centre_moved
    gradient = (
        jnp.stack(
            [
                window(heat_pad, 1, 0, 0) - window(heat_pad, -1, 0, 0),
                window(heat_pad, 0, 1, 0) - window(heat_pad, 0, -1, 0),
                window(heat_pad, 0, 0, 1) - window(heat_pad, 0, 0, -1),
            ],
            0,
        )
        * 0.5
    )
    return (
        centre_heat + time_step * flux,
        centre_moved + time_step * laplace - time_step * coupling * gradient,
    )


def shift_flat(values, offset):
    length = values.shape[-1]
    padding = jnp.zeros(values.shape[:-1] + (abs(offset),), values.dtype)
    if offset > 0:
        return jnp.concatenate([values[..., offset:], padding], -1)
    return jnp.concatenate([padding, values[..., : length + offset]], -1)


def inside_mask(shift_x, shift_y, shift_z):
    position = jnp.arange(EDGE**3, dtype=jnp.int32)
    coord_x = position // (EDGE * EDGE) + shift_x
    coord_y = position // EDGE % EDGE + shift_y
    coord_z = position % EDGE + shift_z
    inside = (
        (coord_x >= 0)
        & (coord_x < EDGE)
        & (coord_y >= 0)
        & (coord_y < EDGE)
        & (coord_z >= 0)
        & (coord_z < EDGE)
    )
    return inside.astype(jnp.float32)


def build_tile(heat_rows, conduct_rows, plastic_rows, refined_rows):
    squared = heat_rows * heat_rows
    factor = 1.0 + 3.0 * refined_rows.astype(jnp.float32)
    stiffness = (
        conduct_rows
        * (1.0 + 0.5 * squared / (1.0 + squared))
        / (1.0 + plastic_rows)
        * factor[:, None]
    )
    entries = []
    for shift_x, shift_y, shift_z, weight in tile_directions():
        offset = shift_x * EDGE * EDGE + shift_y * EDGE + shift_z
        entries.append(
            weight
            * 0.5
            * (stiffness + shift_flat(stiffness, offset))
            * inside_mask(shift_x, shift_y, shift_z)
        )
    return jnp.stack(entries, 1).astype(jnp.bfloat16)


def patch_solve(stencil_tile, fields):
    coeffs = stencil_tile.astype(jnp.float32)
    diagonal = 1.0 + jnp.sum(coeffs, axis=1)
    current = fields
    for smooth_step in range(SMOOTH):
        total = fields
        for number, (shift_x, shift_y, shift_z, weight) in enumerate(tile_directions()):
            offset = shift_x * EDGE * EDGE + shift_y * EDGE + shift_z
            total = total + coeffs[:, number, None, :] * shift_flat(current, offset)
        current = total / diagonal[:, None, :]
    return current


def pad_depth(values):
    return jnp.pad(values, [(0, 0)] * (values.ndim - 1) + [(1, 1)])


def grid_patches(grid_field):
    block_tally = grid_field.shape[2] // EDGE
    blocks = grid_field.reshape(EDGE, EDGE, block_tally, EDGE)
    return blocks.transpose(2, 0, 1, 3).reshape(block_tally, EDGE**3)


def vector_patches(grid_field):
    block_tally = grid_field.shape[3] // EDGE
    blocks = grid_field.reshape(3, EDGE, EDGE, block_tally, EDGE)
    return blocks.transpose(3, 0, 1, 2, 4).reshape(block_tally, 3, EDGE**3)


def routing(owners, capacity, slab_count):
    lane_ids = jnp.arange(owners.shape[0], dtype=jnp.int32)
    earlier = (owners[:, None] == owners[None, :]) & (lane_ids[None, :] < lane_ids[:, None])
    rank_ids = jnp.sum(earlier.astype(jnp.int32), axis=1)
    target = owners * capacity + rank_ids
    buffer_slots = jnp.arange(slab_count * capacity, dtype=jnp.int32)
    matches = buffer_slots[:, None] == target[None, :]
    present = jnp.any(matches, axis=1)
    source = jnp.argmax(matches, axis=1)
    return (present, source)


def pack_rows(rows, present, source, slab_count, capacity, filler):
    gathered_rows = jnp.take(rows, source, axis=0)
    keep_mask = present.reshape((-1,) + (1,) * (rows.ndim - 1))
    packed = jnp.where(keep_mask, gathered_rows, jnp.asarray(filler, rows.dtype))
    return packed.reshape((slab_count, capacity) + rows.shape[1:])


def placement(got_labels, block_tally):
    slot_ids = got_labels.reshape(-1, 2)[:, 0].astype(jnp.int32)
    wanted = jnp.arange(block_tally, dtype=jnp.int32)
    return jnp.argmax(slot_ids[None, :] == wanted[:, None], axis=1)


def take_rows(received, picks):
    flat_rows = received.reshape((-1,) + received.shape[2:])
    return jnp.take(flat_rows, picks, axis=0)


def on_device(
    thermal_level,
    deformation_vector,
    thermal_elastic_modulus,
    yield_strain,
    refinement_flag,
    destination_holder,
    destination_position,
):
    slab_count = lax.axis_size("slab")
    owners = destination_holder.reshape(-1)
    slots = destination_position.reshape(-1)
    refined_rows = refinement_flag.reshape(-1)
    block_tally = owners.shape[0]
    capacity = max(2, 2 * block_tally // slab_count)
    present, source = routing(owners, capacity, slab_count)
    conduct_rows = grid_patches(thermal_elastic_modulus)
    plastic_rows = grid_patches(yield_strain)
    labels = jnp.stack([slots.astype(jnp.float32), refined_rows.astype(jnp.float32)], 1)
    sent_labels = pack_rows(labels, present, source, slab_count, capacity, -1.0)
    conduct_pad = pad_depth(extended(thermal_elastic_modulus, (("slab", 0), ("blk", 1)), 1))
    layered_entries = jnp.concatenate([thermal_level[None], deformation_vector], 0)
    for sweep_index in range(SWEEPS):
        padded = pad_depth(extended(layered_entries, (("slab", 1), ("blk", 2)), 1))
        thermal_state, deformed_state = sweep_core(padded[0], padded[1:], conduct_pad)
        layered_entries = jnp.concatenate([thermal_state[None], deformed_state], 0)
    heat_rows = grid_patches(layered_entries[0])
    moved_rows = vector_patches(layered_entries[1:])
    stencil_tile = build_tile(heat_rows, conduct_rows, plastic_rows, refined_rows)
    got_tile = lax.all_to_all(
        pack_rows(stencil_tile, present, source, slab_count, capacity, 0.0),
        "slab",
        split_axis=0,
        concat_axis=0,
        tiled=True,
    )
    fields = jnp.concatenate([heat_rows[:, None], moved_rows, plastic_rows[:, None]], 1)
    got_fields, got_labels = (
        lax.all_to_all(
            pack_rows(fields, present, source, slab_count, capacity, 0.0),
            "slab",
            split_axis=0,
            concat_axis=0,
            tiled=True,
        ),
        lax.all_to_all(sent_labels, "slab", split_axis=0, concat_axis=0, tiled=True),
    )
    picks = placement(got_labels, block_tally)
    arrived = take_rows(got_fields, picks)
    solved = patch_solve(take_rows(got_tile, picks), arrived[:, 0:4])
    completed_entries = jnp.concatenate([solved, arrived[:, 4:5]], 1)
    volume_sequence = EDGE**3
    relaxed_thermal_entries = completed_entries[:, 0].reshape(1, 1, block_tally, volume_sequence)
    relaxed_deformation_entries = completed_entries[:, 1:4].reshape(
        1, 1, block_tally, 3, volume_sequence
    )
    redistributed_yield_strain = completed_entries[:, 4].reshape(1, 1, block_tally, volume_sequence)
    return (relaxed_thermal_entries, relaxed_deformation_entries, redistributed_yield_strain)


def solution(mesh):
    placed = (
        P("slab", "blk", None),
        P(None, "slab", "blk", None),
        P("slab", "blk", None),
        P("slab", "blk", None),
        P("slab", "blk", None),
        P("slab", "blk", None),
        P("slab", "blk", None),
    )
    return jax.shard_map(
        on_device,
        mesh=mesh,
        in_specs=placed,
        out_specs=(
            P("slab", "blk", None, None),
            P("slab", "blk", None, None, None),
            P("slab", "blk", None, None),
        ),
        check_vma=False,
    )
```

profile of v0, /device:TPU:36, one launch (start us, length us, event | category | flops | bytes accessed | tf_op | source)
XLA Modules:
  0.0 691.3 jit_solution(15319883913735651649)
XLA Ops:
  3.5 3.6 collective-permute-start.1
  18.3 8.8 %all-to-all-start = ((f32[32,2,2]{1,2,0:T(2,128)}), f32[32,2,2]{1,2,0:T(2,128)}, u32[]{:S(2)}, u32[]{:S(2)}) async-start(f32[32,2,2]{1,2,0:T(2,128)} %copy.1084), calls=%async_computation | async-start | bytes 65536 | tf_op jit(solution)/shard_map/all_to_all | solution.py:230
  38.7 4.5 collective-permute-start.7
  48.9 4.3 collective-permute-done.3
  59.0 3.6 collective-permute-start.9
  77.4 4.3 collective-permute-done.11
  87.7 3.6 collective-permute-start.13
  97.3 4.7 collective-permute-done.15
  116.5 4.4 collective-permute-done.19
  128.5 5.6 fusion.2
  167.0 24.2 %stack.204 = bf16[16,26,4096]{2,1,0:T(8,128)(2,1)} concatenate(bf16[16,1,4096]{2,1,0:T(2,128)(2,1)} %copy.1095, bf16[16,1,4096]{2,1,0:T(2,128)(2,1)} %copy.1096, bf16[16,1,4096]{2,1,0:T(2,128)(2,1)} %copy.1097, bf16[16,1,4096]{2,1,0:T(2,128)(2,1)} %copy.1098, bf16[16,1,4096]{2,1,0:T(2,128)(2,1)} %copy.1099, bf16[16,1,4096]{2,1,0:T(2,128)(2,1)} %copy.1100, ...), dimensions={1} | concatenate | bytes 6815744 | tf_op jit(solution)/shard_map/stack | solution.py:123
  191.2 9.9 %gather_fusion.3 = bf16[64,26,4096]{2,1,0:T(8,128)(2,1)} fusion(bf16[16,26,4096]{2,1,0:T(8,128)(2,1)} %stack.204, s32[1024]{0:T(1024)} %copy-done.116), kind=kCustom, calls=%fused_computation.3 | custom fusion | bytes 27263232 | tf_op jit(solution)/shard_map/jit(_take)/gather | solution.py:168
  201.1 3.8 fusion.6
  204.9 4.9 reshape.351
  209.7 7.4 %copy.1191 = f32[3,16,16,16,16]{4,2,1,3,0:T(8,128)} copy(f32[3,16,16,16,16]{4,3,2,1,0:T(8,128)} %reshape.351) | data formatting | bytes 1572864 | tf_op jit(solution)/shard_map/reshape | solution.py:151
  217.1 6.5 reshape.352
  228.6 4.6 gather_fusion.1
  233.2 12.9 %fusion = f32[32,2,5,4096]{3,1,2,0:T(2,128)} fusion(f32[32,2,5,4096]{3,2,1,0:T(8,128)} %bitcast.222, pred[32,2]{1,0:T(8,128)(4,1)S(1)} %broadcast_in_dim.143, pred[32,2]{1,0:T(8,128)(4,1)S(1)} %broadcast_in_dim.141), kind=kLoop, calls=%fused_computation.9 | loop fusion | flops 2621440 | bytes 10485888 | tf_op jit(solution)/shard_map/jit(_where)/select_n | solution.py:170
  246.1 12.7 %all-to-all-start.1 = ((f32[32,2,5,4096]{3,1,2,0:T(2,128)}), f32[32,2,5,4096]{3,1,2,0:T(2,128)}, u32[]{:S(2)}, u32[]{:S(2)}) async-start(f32[32,2,5,4096]{3,1,2,0:T(2,128)} %fusion), calls=%async_computation.1 | async-start | bytes 10485760 | tf_op jit(solution)/shard_map/all_to_all | solution.py:223
  258.8 23.2 %broadcast_select_fusion.1 = bf16[32,2,26,4096]{3,1,2,0:T(2,128)(2,1)} fusion(pred[32,2]{1,0:T(8,128)(4,1)S(1)} %broadcast_in_dim.141, pred[32,2]{1,0:T(8,128)(4,1)S(1)} %broadcast_in_dim.143, bf16[32,2,26,4096]{3,2,1,0:T(8,128)(2,1)} %bitcast.221), kind=kLoop, calls=%fused_computation.6 | loop fusion | flops 13631488 | bytes 27263104 | tf_op jit(solution)/shard_map/jit(_where)/select_n | solution.py:170
  282.0 44.3 %all-to-all-done.1 = f32[32,2,5,4096]{3,1,2,0:T(2,128)} async-done(((f32[32,2,5,4096]{3,1,2,0:T(2,128)}), f32[32,2,5,4096]{3,1,2,0:T(2,128)}, u32[]{:S(2)}, u32[]{:S(2)}) %all-to-all-start.1) | async-done | bytes 5242912 | tf_op jit(solution)/shard_map/all_to_all | solution.py:223
  326.3 7.3 %all-to-all-start.2 = ((bf16[32,2,26,4096]{3,1,2,0:T(2,128)(2,1)}), bf16[32,2,26,4096]{3,1,2,0:T(2,128)(2,1)}, u32[]{:S(2)}, u32[]{:S(2)}) async-start(bf16[32,2,26,4096]{3,1,2,0:T(2,128)(2,1)} %broadcast_select_fusion.1), calls=%async_computation.2 | async-start | bytes 27262976 | tf_op jit(solution)/shard_map/all_to_all | solution.py:214
  333.6 10.4 %copy.1093 = f32[32,2,5,4096]{3,2,1,0:T(8,128)} copy(f32[32,2,5,4096]{3,1,2,0:T(2,128)} %all-to-all-done.1) | data formatting | bytes 10485760 | tf_op jit(solution)/shard_map/all_to_all | solution.py:223
  344.0 5.7 gather_fusion.2
  377.9 175.0 %all-to-all-done.2 = bf16[32,2,26,4096]{3,1,2,0:T(2,128)(2,1)} async-done(((bf16[32,2,26,4096]{3,1,2,0:T(2,128)(2,1)}), bf16[32,2,26,4096]{3,1,2,0:T(2,128)(2,1)}, u32[]{:S(2)}, u32[]{:S(2)}) %all-to-all-start.2) | async-done | bytes 13631520 | tf_op jit(solution)/shard_map/all_to_all | solution.py:214
  552.8 16.9 %copy.1122 = bf16[32,2,26,4096]{3,2,1,0:T(8,128)(2,1)} copy(bf16[32,2,26,4096]{3,1,2,0:T(2,128)(2,1)} %all-to-all-done.2) | data formatting | bytes 27262976 | tf_op jit(solution)/shard_map/all_to_all | solution.py:214
  569.8 8.8 %gather_fusion.4 = bf16[16,26,4096]{2,1,0:T(8,128)(2,1)} fusion(bf16[64,26,4096]{2,1,0:T(8,128)(2,1)} %bitcast.223, s32[1024]{0:T(1024)} %pad_clamp_fusion), kind=kCustom, calls=%fused_computation.4 | custom fusion | bytes 6815808 | tf_op jit(solution)/shard_map/jit(_take)/gather | solution.py:182
  578.5 6.2 select_convert_fusion
  584.7 19.8 %fusion.120 = (f32[16,1,4096]{2,1,0:T(1,128)}, f32[16,1,4096]{2,1,0:T(1,128)S(1)}, f32[16,1,4096]{2,1,0:T(1,128)S(1)}, f32[16,1,4096]{2,1,0:T(1,128)}, f32[16,1,...) fusion(f32[16,26,4096]{2,1,0:T(8,128)} %select_convert_fusion), kind=kLoop, calls=%fused_computation.403 | loop fusion | bytes 9961472 | tf_op jit(solution)/shard_map/slice | solution.py:134
  604.6 9.2 %fusion.121 = (f32[16,1,4096]{2,1,0:T(1,128)}, f32[16,1,4096]{2,1,0:T(1,128)}, f32[16,1,4096]{2,1,0:T(1,128)}, f32[16,1,4096]{2,1,0:T(1,128)}, f32[16,1,4096]{2,...) fusion(f32[16,26,4096]{2,1,0:T(8,128)} %select_convert_fusion), kind=kLoop, calls=%fused_computation.404 | loop fusion | bytes 3670016 | tf_op jit(solution)/shard_map/slice | solution.py:134
  646.7 15.8 %add_divide_fusion.1 = f32[16,4,4096]{2,1,0:T(4,128)S(1)} fusion(f32[16,4,3823]{2,1,0:T(4,128)S(1)} %copy-done.33, f32[16,4,3824]{2,1,0:T(4,128)S(1)} %copy-done.35, f32[16,4,3825]{2,1,0:T(4,128)S(1)} %copy-done.37, f32[16,4,3839]{2,1,0:T(4,128)} %get-tuple-element.127, f32[16,4,3840]{2,1,0:T(4,128)} %get-tuple-element.129, ...), kind=kLoop, calls=%fused_computation.41 | loop fusion | flops 13893632 | bytes 35233280 | tf_op jit(solution)/shard_map/div | solution.py:135
  671.6 16.6 %add_divide_fusion = f32[16,4,4096]{2,1,0:T(4,128)S(1)} fusion(f32[16,4,3823]{2,1,0:T(4,128)S(1)} %get-tuple-element.155, f32[16,4,3824]{2,1,0:T(4,128)S(1)} %get-tuple-element.157, f32[16,4,3825]{2,1,0:T(4,128)S(1)} %get-tuple-element.159, f32[16,4,3839]{2,1,0:T(4,128)S(1)} %get-tuple-element.161, f32[16,4,3840]{2,1,0:T(4,128)S(1)} %get-tuple-element.163, ...), kind=kLoop, calls=%fused_computation.40 | loop fusion | flops 13893632 | bytes 35233280 | tf_op jit(solution)/shard_map/div | solution.py:135
  (454 shorter events, 194.4 us)
Async XLA Ops:
  0.6 42.7 %copy-start.23 = (f32[16,16,256]{2,1,0:T(8,128)S(1)}, f32[16,16,256]{2,1,0:T(8,128)}, u32[]{:S(2)}) copy-start(f32[16,16,256]{2,1,0:T(8,128)} %param.7) | copy-start | bytes 786436
  0.6 42.7 %copy-start.2 = (f32[3,16,16,256]{3,2,1,0:T(8,128)S(1)}, f32[3,16,16,256]{3,2,1,0:T(8,128)}, u32[]{:S(2)}) copy-start(f32[3,16,16,256]{3,2,1,0:T(8,128)} %param.8) | copy-start | bytes 2359300
  1.6 41.7 %collective-permute-start = (f32[4,1,16,256]{3,2,1,0:T(8,128)S(1)}, f32[4,1,16,256]{3,2,1,0:T(8,128)S(1)}, u32[]{:S(2)}, u32[]{:S(2)}) collective-permute-start(f32[4,1,16,256]{3,2,1,0:T(8,128)S(1)} %get-tuple-element.186), channel_id=1, source_target_pairs={{0,4},{4,8},{8,12},{12,16},{16,20},{20,24},{24,28},{28,32},{32,36}... | collective-permute-start | bytes 196616 | tf_op jit(solution)/shard_map/ppermute | solution.py:20
  3.5 39.8 %collective-permute-start.1 = (f32[4,1,16,256]{3,2,1,0:T(8,128)S(1)}, f32[4,1,16,256]{3,2,1,0:T(8,128)S(1)}, u32[]{:S(2)}, u32[]{:S(2)}) collective-permute-start(f32[4,1,16,256]{3,2,1,0:T(8,128)S(1)} %get-tuple-element.187), channel_id=1, source_target_pairs={{4,0},{8,4},{12,8},{16,12},{20,16},{24,20},{28,24},{32,28},{36,32}... | collective-permute-start | bytes 196616 | tf_op jit(solution)/shard_map/ppermute | solution.py:23
  7.9 28.5 %collective-permute-start.5 = (f32[1,16,256]{2,1,0:T(8,128)S(1)}, f32[1,16,256]{2,1,0:T(8,128)S(1)}, u32[]{:S(2)}, u32[]{:S(2)}) collective-permute-start(f32[1,16,256]{2,1,0:T(8,128)S(1)} %get-tuple-element.254), channel_id=1, source_target_pairs={{0,4},{4,8},{8,12},{12,16},{16,20},{20,24},{24,28},{28,32},{32,36}... | collective-permute-start | bytes 49160 | tf_op jit(solution)/shard_map/ppermute | solution.py:20
  10.1 27.3 %collective-permute-start.4 = (f32[1,16,256]{2,1,0:T(8,128)S(1)}, f32[1,16,256]{2,1,0:T(8,128)S(1)}, u32[]{:S(2)}, u32[]{:S(2)}) collective-permute-start(f32[1,16,256]{2,1,0:T(8,128)S(1)} %get-tuple-element.255), channel_id=1, source_target_pairs={{4,0},{8,4},{12,8},{16,12},{20,16},{24,20},{28,24},{32,28},{36,32}... | collective-permute-start | bytes 49160 | tf_op jit(solution)/shard_map/ppermute | solution.py:23
  18.3 52.6 %all-to-all-start = ((f32[32,2,2]{1,2,0:T(2,128)}), f32[32,2,2]{1,2,0:T(2,128)}, u32[]{:S(2)}, u32[]{:S(2)}) async-start(f32[32,2,2]{1,2,0:T(2,128)} %copy.1084), calls=%async_computation | async-start | bytes 65536 | tf_op jit(solution)/shard_map/all_to_all | solution.py:230
  37.4 10.8 %collective-permute-start.6 = (f32[18,1,256]{2,1,0:T(1,128)S(1)}, f32[18,1,256]{2,1,0:T(1,128)S(1)}, u32[]{:S(2)}, u32[]{:S(2)}) collective-permute-start(f32[18,1,256]{2,1,0:T(1,128)S(1)} %get-tuple-element.201), channel_id=1, source_target_pairs={{1,0},{2,1},{3,2},{5,4},{6,5},{7,6},{9,8},{10,9},{11,10},{13,12},{... | collective-permute-start | bytes 55304 | tf_op jit(solution)/shard_map/ppermute | solution.py:23
  38.7 9.5 %collective-permute-start.7 = (f32[18,1,256]{2,1,0:T(1,128)S(1)}, f32[18,1,256]{2,1,0:T(1,128)S(1)}, u32[]{:S(2)}, u32[]{:S(2)}) collective-permute-start(f32[18,1,256]{2,1,0:T(1,128)S(1)} %get-tuple-element.200), channel_id=1, source_target_pairs={{0,1},{1,2},{2,3},{4,5},{5,6},{6,7},{8,9},{9,10},{10,11},{12,13},{... | collective-permute-start | bytes 55304 | tf_op jit(solution)/shard_map/ppermute | solution.py:20
  43.5 5.5 collective-permute-start.2
  46.9 6.2 collective-permute-start.3
  57.0 14.9 %collective-permute-start.8 = (f32[4,1,16,256]{3,2,1,0:T(8,128)S(1)}, f32[4,1,16,256]{3,2,1,0:T(8,128)S(1)}, u32[]{:S(2)}, u32[]{:S(2)}) collective-permute-start(f32[4,1,16,256]{3,2,1,0:T(8,128)S(1)} %get-tuple-element.184), channel_id=1, source_target_pairs={{0,4},{4,8},{8,12},{12,16},{16,20},{20,24},{24,28},{28,32},{32,36}... | collective-permute-start | bytes 196616 | tf_op jit(solution)/shard_map/ppermute | solution.py:20
  59.0 12.8 %collective-permute-start.9 = (f32[4,1,16,256]{3,2,1,0:T(8,128)S(1)}, f32[4,1,16,256]{3,2,1,0:T(8,128)S(1)}, u32[]{:S(2)}, u32[]{:S(2)}) collective-permute-start(f32[4,1,16,256]{3,2,1,0:T(8,128)S(1)} %get-tuple-element.185), channel_id=1, source_target_pairs={{4,0},{8,4},{12,8},{16,12},{20,16},{24,20},{28,24},{32,28},{36,32}... | collective-permute-start | bytes 196616 | tf_op jit(solution)/shard_map/ppermute | solution.py:23
  72.0 5.5 collective-permute-start.10
  75.5 6.2 collective-permute-start.11
  85.8 6.2 collective-permute-start.12
  87.7 5.5 collective-permute-start.13
  93.3 4.0 collective-permute-start.14
  95.3 6.7 collective-permute-start.15
  105.3 6.1 collective-permute-start.16
  107.4 5.4 collective-permute-start.17
  112.9 3.6 collective-permute-start.18
  114.5 6.4 collective-permute-start.19
  246.1 80.2 %all-to-all-start.1 = ((f32[32,2,5,4096]{3,1,2,0:T(2,128)}), f32[32,2,5,4096]{3,1,2,0:T(2,128)}, u32[]{:S(2)}, u32[]{:S(2)}) async-start(f32[32,2,5,4096]{3,1,2,0:T(2,128)} %fusion), calls=%async_computation.1 | async-start | bytes 10485760 | tf_op jit(solution)/shard_map/all_to_all | solution.py:223
  326.3 226.6 %all-to-all-start.2 = ((bf16[32,2,26,4096]{3,1,2,0:T(2,128)(2,1)}), bf16[32,2,26,4096]{3,1,2,0:T(2,128)(2,1)}, u32[]{:S(2)}, u32[]{:S(2)}) async-start(bf16[32,2,26,4096]{3,1,2,0:T(2,128)(2,1)} %broadcast_select_fusion.1), calls=%async_computation.2 | async-start | bytes 27262976 | tf_op jit(solution)/shard_map/all_to_all | solution.py:214
  604.6 41.9 %copy-start.35 = (f32[16,4,3824]{2,1,0:T(4,128)S(1)}, f32[16,4,3824]{2,1,0:T(4,128)}, u32[]{:S(2)}) copy-start(f32[16,4,3824]{2,1,0:T(4,128)} %get-tuple-element.123) | copy-start | bytes 2936836
  604.6 41.9 %copy-start.36 = (f32[16,4,3825]{2,1,0:T(4,128)S(1)}, f32[16,4,3825]{2,1,0:T(4,128)}, u32[]{:S(2)}) copy-start(f32[16,4,3825]{2,1,0:T(4,128)} %get-tuple-element.124) | copy-start | bytes 2937604
  604.6 41.9 %copy-start.37 = (f32[16,4,3825]{2,1,0:T(4,128)S(1)}, f32[16,4,3825]{2,1,0:T(4,128)}, u32[]{:S(2)}) copy-start(f32[16,4,3825]{2,1,0:T(4,128)} %get-tuple-element.125) | copy-start | bytes 2937604
  604.6 41.9 %copy-start.38 = (f32[16,4,3839]{2,1,0:T(4,128)S(1)}, f32[16,4,3839]{2,1,0:T(4,128)}, u32[]{:S(2)}) copy-start(f32[16,4,3839]{2,1,0:T(4,128)} %get-tuple-element.126) | copy-start | bytes 2948356
  613.8 32.7 %copy-start.31 = (f32[16,4,3857]{2,1,0:T(4,128)S(1)}, f32[16,4,3857]{2,1,0:T(4,128)}, u32[]{:S(2)}) copy-start(f32[16,4,3857]{2,1,0:T(4,128)} %get-tuple-element.137) | copy-start | bytes 2962180
  613.8 32.7 %copy-start.32 = (f32[16,4,3823]{2,1,0:T(4,128)S(1)}, f32[16,4,3823]{2,1,0:T(4,128)}, u32[]{:S(2)}) copy-start(f32[16,4,3823]{2,1,0:T(4,128)} %get-tuple-element.120) | copy-start | bytes 2936068
  613.8 32.7 %copy-start.33 = (f32[16,4,3823]{2,1,0:T(4,128)S(1)}, f32[16,4,3823]{2,1,0:T(4,128)}, u32[]{:S(2)}) copy-start(f32[16,4,3823]{2,1,0:T(4,128)} %get-tuple-element.121) | copy-start | bytes 2936068
  (109 other events, 1178.9 us)
where the time goes:
time: 702 us; the launch traced here: 691 us
  local copies, waits for them, and re-layouts  246 us (35%)
  waiting for transfers between devices  241 us (34%)
  other arithmetic  122 us (17%)
  starting transfers between devices  78.5 us (11%)
    all_to_all x1, waiting for transfers between devices, on_device(): lax.all_to_all(pack_rows(stencil_tile, present, source, slab_count, capac...  175 us
    another operation x27, local copies, waits for them, and re-layouts, build_tile(): return jnp.stack(entries, 1).astype(jnp.bfloat16)  47.6 us
    all_to_all x1, waiting for transfers between devices, on_device(): lax.all_to_all(pack_rows(fields, present, source, slab_count, capacity, 0...  44.3 us
    unnamed x267, local copies, waits for them, and re-layouts  38.5 us
    select_n x3, other arithmetic, pack_rows(): jnp.where(keep_mask, gathered_rows, jnp.asarray(filler, rows.dtype))  36.1 us
    slice x26, local copies, waits for them, and re-layouts, shift_flat(): return jnp.concatenate([padding, values[..., :length + offset]], -1)  32.6 us
    div x2, other arithmetic, patch_solve(): current = total / diagonal[:, None, :]  32.4 us
    slice x2, local copies, waits for them, and re-layouts, patch_solve(): total = total + coeffs[:, number, None, :] * shift_flat(current, offset)  29 us
  transfers between devices with their start and end apart: 23, of which 12 were waited for; matrix products, arithmetic and copies ran while one was open for 14% of the time, Pallas kernels for 0%

commit v1 on v0

v1 whole, which is shorter than its diff:
```python
import jax
import jax.numpy as jnp
from jax import lax
from jax.experimental import pallas as pl
from jax.experimental.pallas import tpu as pltpu
from jax.sharding import PartitionSpec as P

EDGE = 16
DEPTH = 256
SWEEPS = 4
N_SLAB = 32
N_BLK = 4
P_DEV = 16
ROWS = N_SLAB * P_DEV
MESH = pl.DeviceIdType.MESH
F32 = jnp.float32
I32 = jnp.int32
BF16 = jnp.bfloat16

PLASTIC_LOW = 0.2235
PLASTIC_STEPS = 65535.0 / (1.4145 - PLASTIC_LOW)

OFFSETS = [
    (dx, dy, dz)
    for dx in (-1, 0, 1)
    for dy in (-1, 0, 1)
    for dz in (-1, 0, 1)
    if (dx, dy, dz) != (0, 0, 0)
]
WEIGHTS = [0.0, 0.1, 0.04, 0.02]


def plane_number(dy, dz):
    return (dy + 1) * 3 + dz + 1


def lane_of(shape):
    return lax.broadcasted_iota(I32, shape, 1)


def row_of(shape):
    return lax.broadcasted_iota(I32, shape, 0)


def shifted_planes(plane, row, inner):
    below = jnp.where(inner == 0, 0.0, pltpu.roll(plane, 1, 1))
    above = jnp.where(inner == EDGE - 1, 0.0, pltpu.roll(plane, DEPTH - 1, 1))
    three = (below, plane, above)
    low = [jnp.where(row == 0, 0.0, pltpu.roll(part, 1, 0)) for part in three]
    high = [jnp.where(row == EDGE - 1, 0.0, pltpu.roll(part, EDGE - 1, 0)) for part in three]
    return low + list(three) + high


def swap_rows_and_groups(tile, row, group):
    for bit in (4, 2, 1):
        row_bit = (row & bit) != 0
        group_bit = (group & bit) != 0
        down = pltpu.roll(pltpu.roll(tile, bit, 0), 128 - 16 * bit, 1)
        up = down if bit == 4 else pltpu.roll(pltpu.roll(tile, 8 - bit, 0), 16 * bit, 1)
        tile = jnp.where(row_bit == group_bit, tile, jnp.where(row_bit, down, up))
    return tile


def byte_of(words, number):
    part = words if number == 0 else lax.shift_right_logical(words, 8 * number)
    return (part & 255).astype(F32).astype(BF16)


def joined(low, high):
    return (low + 256.0 * high).astype(I32)


def move_kernel(
    thermal, deform, modulus, plastic, flag, holder, position,
    out_words, out_plastic, out_exponents,
    state, halo_y, stage_y, cond, cond_y, cond_stage,
    face_x, face_ym, face_yp, face_zm, face_zp, centre,
    stiff, weights, tile, inverse, values,
    send_one, recv_one, send_two, plastic_one, plastic_got, plastic_two,
    one_hot, table, plastic_table,
    load_sem, x_send, x_recv, y_send, y_recv,
    one_send, one_recv, two_send, two_recv, pl_one_send, pl_one_recv, pl_two_send, pl_two_recv, own_sem,
):
    s = lax.axis_index("slab")
    b = lax.axis_index("blk")
    up, down = lax.rem(s + 1, N_SLAB), lax.rem(s + N_SLAB - 1, N_SLAB)
    right, left = lax.rem(b + 1, N_BLK), lax.rem(b + N_BLK - 1, N_BLK)
    has_up, has_down = s < N_SLAB - 1, s > 0
    has_right, has_left = b < N_BLK - 1, b > 0

    loads = [
        pltpu.make_async_copy(thermal, state.at[0, 0, pl.ds(1, EDGE)], load_sem.at[0]),
        pltpu.make_async_copy(deform, state.at[0, pl.ds(1, 3), pl.ds(1, EDGE)], load_sem.at[1]),
        pltpu.make_async_copy(modulus, cond.at[pl.ds(1, EDGE)], load_sem.at[2]),
    ]
    for load in loads:
        load.start()

    barrier = pltpu.get_barrier_semaphore()

    def greet(step, carry):
        peer = lax.rem(s + step, N_SLAB)
        pl.semaphore_signal(barrier, inc=1, device_id=(peer, b), device_id_type=MESH)
        return carry

    lax.fori_loop(1, N_SLAB, greet, 0)

    @pl.when(has_right)
    def _():
        pl.semaphore_signal(barrier, inc=1, device_id=(s, right), device_id_type=MESH)

    @pl.when(has_left)
    def _():
        pl.semaphore_signal(barrier, inc=1, device_id=(s, left), device_id_type=MESH)

    zero_plane = jnp.zeros((EDGE, DEPTH), F32)

    for has, place, side in ((has_down, 0, 0), (has_up, EDGE + 1, 1)):

        @pl.when(jnp.logical_not(has))
        def _():
            cond[place] = zero_plane
            for t in range(SWEEPS):
                for f in range(4):
                    state[t, f, place] = zero_plane

    for has, side in ((has_left, 0), (has_right, 1)):

        @pl.when(jnp.logical_not(has))
        def _():
            cond_y[side] = zero_plane
            for t in range(SWEEPS):
                for f in range(4):
                    halo_y[t, side, f] = zero_plane

    neighbours = 31 + has_right.astype(I32) + has_left.astype(I32)
    pl.semaphore_wait(barrier, neighbours)

    def x_copies(kind):
        out = []
        for direction, peer in ((0, down), (1, up)):
            mine = 0 if direction == 0 else EDGE - 1
            there = EDGE + 1 if direction == 0 else 0
            if kind == 0:
                source, target = thermal.at[mine], state.at[0, 0, there]
            elif kind == 4:
                source, target = deform.at[:, mine], state.at[0, pl.ds(1, 3), there]
            elif kind == 5:
                source, target = modulus.at[mine], cond.at[there]
            else:
                source, target = state.at[kind, :, mine + 1], state.at[kind, :, there]
            out.append(
                pltpu.make_async_remote_copy(
                    source, target, x_send.at[kind, direction], x_recv.at[kind, direction],
                    device_id=(peer, b), device_id_type=MESH,
                )
            )
        return out

    def y_copies(kind):
        out = []
        for direction, peer in ((0, left), (1, right)):
            if kind == 4:
                source, target = cond_stage.at[direction], cond_y.at[1 - direction]
            else:
                source, target = stage_y.at[kind, direction], halo_y.at[kind, 1 - direction]
            out.append(
                pltpu.make_async_remote_copy(
                    source, target, y_send.at[kind, direction], y_recv.at[kind, direction],
                    device_id=(s, peer), device_id_type=MESH,
                )
            )
        return out

    def start(copies, to_low, to_high):
        @pl.when(to_low)
        def _():
            copies[0].start()

        @pl.when(to_high)
        def _():
            copies[1].start()

    def wait_recv(copies, from_high, from_low):
        @pl.when(from_high)
        def _():
            copies[0].wait_recv()

        @pl.when(from_low)
        def _():
            copies[1].wait_recv()

    def wait_send(copies, to_low, to_high):
        @pl.when(to_low)
        def _():
            copies[0].wait_send()

        @pl.when(to_high)
        def _():
            copies[1].wait_send()

    for kind in (5, 0, 4):
        start(x_copies(kind), has_down, has_up)
    for load in loads:
        load.wait()

    def stage_first(x, carry):
        for side, y in ((0, 0), (1, EDGE - 1)):
            cond_stage[side, pl.ds(x, 1), :] = cond[x + 1, y : y + 1, :]
            for f in range(4):
                stage_y[0, side, f, pl.ds(x, 1), :] = state[0, f, x + 1, y : y + 1, :]
        return carry

    lax.fori_loop(0, EDGE, stage_first, 0)
    start(y_copies(4), has_left, has_right)
    start(y_copies(0), has_left, has_right)

    row8 = row_of((8, 128))
    group8 = lane_of((8, 128)) // EDGE
    row = row_of((EDGE, DEPTH))
    lane = lane_of((EDGE, DEPTH))
    inner = lane & (EDGE - 1)

    slot_lane = lane_of((1, 128))
    slot_row = jnp.zeros((1, 128), I32)
    for p in range(P_DEV):
        code = holder[0, 0, p] * P_DEV + position[0, 0, p]
        slot_row = jnp.where(slot_lane == lax.rem(s, 8) * P_DEV + p, code, slot_row)

    def plastic_out(step, carry):
        x = lax.rem(step + s // 2, EDGE)
        root = plastic[x]
        root = root * lax.rsqrt(root)
        codes = jnp.clip((root - PLASTIC_LOW) * PLASTIC_STEPS + 0.5, 0.0, 65535.0).astype(I32)
        words = (codes[:, 0:128] << 16) | codes[:, 128:256]
        for half in range(2):
            m = 2 * x + half
            plastic_one[m, 0:8, :] = swap_rows_and_groups(words[8 * half : 8 * half + 8], row8, group8)
            plastic_one[m, 8:9, :] = slot_row

            @pl.when(m != s)
            def _():
                pltpu.make_async_remote_copy(
                    plastic_one.at[m, pl.ds(0, 9)], plastic_got.at[s, pl.ds(0, 9)], pl_one_send, pl_one_recv,
                    device_id=(m, b), device_id_type=MESH,
                ).start()

            @pl.when(m == s)
            def _():
                plastic_got[s, 0:9, :] = plastic_one[m, 0:9, :]

        return carry

    lax.fori_loop(0, EDGE, plastic_out, 0)

    for dy in (-1, 0, 1):
        for dz in (-1, 0, 1):
            inside = (row + dy >= 0) & (row + dy < EDGE) & (inner + dz >= 0) & (inner + dz < EDGE)
            reach = abs(dy) + abs(dz)
            weights[0, plane_number(dy, dz)] = jnp.where(inside, 0.5 * WEIGHTS[reach], 0.0)
            weights[1, plane_number(dy, dz)] = jnp.where(inside, 0.5 * WEIGHTS[reach + 1], 0.0)
    for n in range(9):
        for place in (0, EDGE + 1):
            stiff[n, place] = zero_plane
            for k in range(2):
                for f in range(4):
                    values[k, f, n, place] = zero_plane

    factor = jnp.ones((1, DEPTH), F32)
    lane_row = lane_of((1, DEPTH)) // EDGE
    for p in range(P_DEV):
        factor = jnp.where(lane_row == p, 1.0 + 3.0 * flag[0, 0, p].astype(F32), factor)

    wait_recv(x_copies(5), has_up, has_down)
    wait_recv(y_copies(4), has_right, has_left)

    def face(x, carry):
        here = cond[x + 1]
        ym = jnp.where(row == 0, cond_y[0, pl.ds(x, 1), :], pltpu.roll(here, 1, 0))
        yp = jnp.where(row == EDGE - 1, cond_y[1, pl.ds(x, 1), :], pltpu.roll(here, EDGE - 1, 0))
        zm = jnp.where(lane == 0, 0.0, pltpu.roll(here, 1, 1))
        zp = jnp.where(lane == DEPTH - 1, 0.0, pltpu.roll(here, DEPTH - 1, 1))
        low = 0.06 * (cond[x] + here)
        high = 0.06 * (here + cond[x + 2])
        face_x[x] = low
        face_x[x + 1] = high
        ym, yp, zm, zp = (0.06 * (here + beside) for beside in (ym, yp, zm, zp))
        face_ym[x] = ym
        face_yp[x] = yp
        face_zm[x] = zm
        face_zp[x] = zp
        centre[x] = 1.0 - (low + high + ym + yp + zm + zp)
        return carry

    lax.fori_loop(0, EDGE, face, 0)

    def sweep_plane(t, x):
        around = []
        for f in range(4):
            here = state[t, f, x + 1]
            around.append(
                (
                    here,
                    state[t, f, x],
                    state[t, f, x + 2],
                    jnp.where(row == 0, halo_y[t, 0, f, pl.ds(x, 1), :], pltpu.roll(here, 1, 0)),
                    jnp.where(row == EDGE - 1, halo_y[t, 1, f, pl.ds(x, 1), :], pltpu.roll(here, EDGE - 1, 0)),
                    jnp.where(lane == 0, 0.0, pltpu.roll(here, 1, 1)),
                    jnp.where(lane == DEPTH - 1, 0.0, pltpu.roll(here, DEPTH - 1, 1)),
                )
            )
        h, xm, xp, ym, yp, zm, zp = around[0]
        fresh = [
            centre[x] * h
            + face_x[x] * xm
            + face_x[x + 1] * xp
            + face_ym[x] * ym
            + face_yp[x] * yp
            + face_zm[x] * zm
            + face_zp[x] * zp
        ]
        slopes = (xp - xm, yp - ym, zp - zm)
        for c in range(3):
            u, *six = around[c + 1]
            total = (six[0] + six[1]) + (six[2] + six[3]) + (six[4] + six[5])
            fresh.append(0.28 * u + 0.12 * total - 0.06 * slopes[c])
        for f in range(4):
            state[t + 1, f, x + 1] = fresh[f]
            if t + 1 < SWEEPS:
                stage_y[t + 1, 0, f, pl.ds(x, 1), :] = fresh[f][0:1]
                stage_y[t + 1, 1, f, pl.ds(x, 1), :] = fresh[f][EDGE - 1 : EDGE]

    def sweep(t):
        def middle(x, carry):
            sweep_plane(t, x)
            return carry

        if t + 1 < SWEEPS:
            sweep_plane(t, 0)
            sweep_plane(t, EDGE - 1)
            start(x_copies(t + 1), has_down, has_up)
            lax.fori_loop(1, EDGE - 1, middle, 0)
            start(y_copies(t + 1), has_left, has_right)
        else:
            lax.fori_loop(0, EDGE, middle, 0)

    wait_recv(x_copies(0), has_up, has_down)
    wait_recv(x_copies(4), has_up, has_down)
    wait_recv(y_copies(0), has_right, has_left)
    sweep(0)

    def wait_all(ref, semaphore):
        pltpu.make_async_copy(ref, ref, semaphore).wait()

    wait_all(plastic_got.at[pl.ds(0, N_SLAB - 1), pl.ds(0, 9)], pl_one_recv)
    slot_id = row_of((ROWS, 128))
    for g in range(4):
        codes = plastic_got[8 * g, 8:9, :]
        for k in range(1, 8):
            codes = codes + plastic_got[8 * g + k, 8:9, :]
        one_hot[:, 128 * g : 128 * g + 128] = jnp.where(slot_id == codes, 1.0, 0.0).astype(BF16)

    def plastic_unpack(g, carry):
        words = plastic_got[pl.ds(4 * g, 4), 0:8, :]
        both = jnp.concatenate([lax.shift_right_logical(words, 16), words & 65535], axis=1).reshape(64, 128)
        place = pl.ds(pl.multiple_of(64 * g, 64), 64)
        plastic_table[place, 0:128] = byte_of(both, 0)
        plastic_table[place, 128:256] = byte_of(both, 1)
        return carry

    lax.fori_loop(0, 8, plastic_unpack, 0)

    def plastic_on(step, carry):
        g = lax.rem(step + s // 8, 4)
        place = pl.ds(pl.multiple_of(128 * g, 128), 128)
        rows = jnp.dot(one_hot[place, :], plastic_table[...], preferred_element_type=F32)
        codes = joined(rows[:, 0:128], rows[:, 128:256]).reshape(8, P_DEV, 128)
        plastic_two[pl.ds(8 * g, 8)] = (codes[:, 0:8] << 16) | codes[:, 8:16]
        for k in range(8):
            d = 8 * g + lax.rem(s + k, 8)

            @pl.when(d != s)
            def _():
                pltpu.make_async_remote_copy(
                    plastic_two.at[d], out_plastic.at[s], pl_two_send, pl_two_recv,
                    device_id=(d, b), device_id_type=MESH,
                ).start()

            @pl.when(d == s)
            def _():
                pltpu.make_async_copy(plastic_two.at[d], out_plastic.at[s], own_sem.at[0]).start()

        return carry

    lax.fori_loop(0, 4, plastic_on, 0)

    for t in range(1, SWEEPS):
        wait_recv(x_copies(t), has_up, has_down)
        wait_recv(y_copies(t), has_right, has_left)
        sweep(t)

    def prepare(x, most):
        fields = [state[SWEEPS, f, x + 1] for f in range(4)]
        squared = fields[0] * fields[0]
        stiffness = cond[x + 1] * (1.0 + 0.5 * squared / (1.0 + squared)) / (1.0 + plastic[x]) * factor
        for n, plane in enumerate(shifted_planes(stiffness, row, inner)):
            stiff[n, x + 1] = plane
        for f in range(4):
            for n, plane in enumerate(shifted_planes(fields[f], row, inner)):
                values[0, f, n, x + 1] = plane
        return tuple(jnp.maximum(most[f], jnp.abs(fields[f])) for f in range(4))

    most = lax.fori_loop(0, EDGE, prepare, (zero_plane,) * 4)
    exponents = []
    exponent_row = jnp.zeros((1, 128), I32)
    scales = []
    for f in range(4):
        largest = jnp.max(jnp.max(most[f], axis=0, keepdims=True), axis=1, keepdims=True)
        exponent = jnp.ceil(jnp.log2(jnp.maximum(largest, 1e-30)) + 0.001)
        scales.append(jnp.exp2(-exponent))
        exponent_row = jnp.where(slot_lane == f, exponent.astype(I32), exponent_row)

    def build(x, carry):
        own = stiff[4, x + 1]
        total = jnp.ones((EDGE, DEPTH), F32)
        for number, (dx, dy, dz) in enumerate(OFFSETS):
            n = plane_number(dy, dz)
            weight = weights[abs(dx), n]
            entry = weight * (own + stiff[n, x + 1 + dx])
            if dx < 0:
                entry = entry * (x > 0).astype(F32)
            if dx > 0:
                entry = entry * (x < EDGE - 1).astype(F32)
            entry = entry.astype(BF16).astype(F32)
            tile[number, x] = entry
            total = total + entry
        inverse[x] = 1.0 / total
        return carry

    lax.fori_loop(0, EDGE, build, 0)

    def smoothed(k, x):
        totals = [state[SWEEPS, f, x + 1] for f in range(4)]
        for number, (dx, dy, dz) in enumerate(OFFSETS):
            entry = tile[number, x]
            for f in range(4):
                totals[f] = totals[f] + entry * values[k, f, plane_number(dy, dz), x + 1 + dx]
        scale = inverse[x]
        return [total * scale for total in totals]

    def first(x, carry):
        fields = smoothed(0, x)
        for f in range(4):
            for n, plane in enumerate(shifted_planes(fields[f], row, inner)):
                values[1, f, n, x + 1] = plane
        return carry

    lax.fori_loop(0, EDGE, first, 0)

    def second(step, carry):
        x = lax.rem(step + s // 2, EDGE)
        codes = []
        for f, field in enumerate(smoothed(1, x)):
            part = jnp.abs(field) * scales[f]
            part = jnp.minimum(part * lax.rsqrt(part + 1e-37), 1.0) * 32767.0
            codes.append((jnp.where(field < 0.0, -part, part) + 32768.5).astype(I32))
        words = [(codes[0] << 16) | codes[1], (codes[2] << 16) | codes[3]]
        for half in range(2):
            m = 2 * x + half
            for w in range(2):
                for side in range(2):
                    part = words[w][8 * half : 8 * half + 8, 128 * side : 128 * side + 128]
                    place = 16 * w + 8 * side
                    send_one[m, place : place + 8, :] = swap_rows_and_groups(part, row8, group8)
            send_one[m, 32:33, :] = exponent_row

            @pl.when(m != s)
            def _():
                pltpu.make_async_remote_copy(
                    send_one.at[m, pl.ds(0, 33)], recv_one.at[s, pl.ds(0, 33)], one_send, one_recv,
                    device_id=(m, b), device_id_type=MESH,
                ).start()

            @pl.when(m == s)
            def _():
                recv_one[s, 0:33, :] = send_one[m, 0:33, :]

        return carry

    lax.fori_loop(0, EDGE, second, 0)
    wait_all(recv_one.at[pl.ds(0, N_SLAB - 1), pl.ds(0, 33)], one_recv)

    def unpack(g, carry):
        place = pl.ds(pl.multiple_of(64 * g, 64), 64)
        for w in range(2):
            words = recv_one[pl.ds(4 * g, 4), 16 * w : 16 * w + 16, :].reshape(64, 128)
            for number in range(4):
                at = 128 * (4 * w + number)
                table[place, at : at + 128] = byte_of(words, number)
        return carry

    lax.fori_loop(0, 8, unpack, 0)

    def onward(step, carry):
        g = lax.rem(step + s // 8, 4)
        place = pl.ds(pl.multiple_of(128 * g, 128), 128)
        rows = jnp.dot(one_hot[place, :], table[...], preferred_element_type=F32)
        for w in range(2):
            parts = [rows[:, 128 * (4 * w + n) : 128 * (4 * w + n) + 128] for n in range(4)]
            words = joined(parts[0], parts[1]) | (joined(parts[2], parts[3]) << 16)
            send_two[pl.ds(8 * g, 8), 16 * w : 16 * w + 16, :] = words.reshape(8, P_DEV, 128)
        for k in range(8):
            d = 8 * g + lax.rem(s + k, 8)

            @pl.when(d != s)
            def _():
                pltpu.make_async_remote_copy(
                    send_two.at[d], out_words.at[s], two_send, two_recv,
                    device_id=(d, b), device_id_type=MESH,
                ).start()

            @pl.when(d == s)
            def _():
                pltpu.make_async_copy(send_two.at[d], out_words.at[s], own_sem.at[1]).start()

        return carry

    lax.fori_loop(0, 4, onward, 0)

    sources = jnp.concatenate(
        [jnp.broadcast_to(recv_one[k, 32:33, :].astype(F32), (P_DEV, 128)) for k in range(N_SLAB)], axis=0
    ).astype(BF16)
    mine = one_hot[pl.ds(pl.multiple_of(s * P_DEV, P_DEV), P_DEV), :]
    out_exponents[...] = jnp.dot(mine, sources, preferred_element_type=F32)

    for kind in (0, 1, 2, 3, 4, 5):
        wait_send(x_copies(kind), has_down, has_up)
    for kind in (0, 1, 2, 3, 4):
        wait_send(y_copies(kind), has_left, has_right)
    wait_all(plastic_one.at[pl.ds(0, N_SLAB - 1), pl.ds(0, 9)], pl_one_send)
    wait_all(send_one.at[pl.ds(0, N_SLAB - 1), pl.ds(0, 33)], one_send)
    wait_all(plastic_two.at[pl.ds(0, N_SLAB - 1)], pl_two_send)
    wait_all(send_two.at[pl.ds(0, N_SLAB - 1)], two_send)
    pltpu.make_async_copy(plastic_two.at[s], out_plastic.at[s], own_sem.at[0]).wait()
    pltpu.make_async_copy(send_two.at[s], out_words.at[s], own_sem.at[1]).wait()
    wait_all(out_plastic.at[pl.ds(0, N_SLAB - 1)], pl_two_recv)
    wait_all(out_words.at[pl.ds(0, N_SLAB - 1)], two_recv)


def move(thermal, deform, modulus, plastic, flag, holder, position):
    anywhere = pl.BlockSpec(memory_space=pl.ANY)
    vmem = pl.BlockSpec(memory_space=pltpu.VMEM)
    smem = pl.BlockSpec(memory_space=pltpu.SMEM)
    plane = (EDGE, DEPTH)
    dma = pltpu.SemaphoreType.DMA
    return pl.pallas_call(
        move_kernel,
        name="sweep_solve_move",
        out_shape=(
            jax.ShapeDtypeStruct((N_SLAB, 32, 128), I32),
            jax.ShapeDtypeStruct((N_SLAB, 8, 128), I32),
            jax.ShapeDtypeStruct((P_DEV, 128), F32),
        ),
        in_specs=[anywhere, anywhere, anywhere, vmem, smem, smem, smem],
        out_specs=(anywhere, anywhere, vmem),
        scratch_shapes=[
            pltpu.VMEM((SWEEPS + 1, 4, EDGE + 2) + plane, F32),
            pltpu.VMEM((SWEEPS, 2, 4) + plane, F32),
            pltpu.VMEM((SWEEPS, 2, 4) + plane, F32),
            pltpu.VMEM((EDGE + 2,) + plane, F32),
            pltpu.VMEM((2,) + plane, F32),
            pltpu.VMEM((2,) + plane, F32),
            pltpu.VMEM((EDGE + 1,) + plane, F32),
            pltpu.VMEM((EDGE,) + plane, F32),
            pltpu.VMEM((EDGE,) + plane, F32),
            pltpu.VMEM((EDGE,) + plane, F32),
            pltpu.VMEM((EDGE,) + plane, F32),
            pltpu.VMEM((EDGE,) + plane, F32),
            pltpu.VMEM((9, EDGE + 2) + plane, F32),
            pltpu.VMEM((2, 9) + plane, F32),
            pltpu.VMEM((26, EDGE) + plane, F32),
            pltpu.VMEM((EDGE,) + plane, F32),
            pltpu.VMEM((2, 4, 9, EDGE + 2) + plane, F32),
            pltpu.VMEM((N_SLAB, 40, 128), I32),
            pltpu.VMEM((N_SLAB, 40, 128), I32),
            pltpu.VMEM((N_SLAB, 32, 128), I32),
            pltpu.VMEM((N_SLAB, 16, 128), I32),
            pltpu.VMEM((N_SLAB, 16, 128), I32),
            pltpu.VMEM((N_SLAB, 8, 128), I32),
            pltpu.VMEM((ROWS, ROWS), BF16),
            pltpu.VMEM((ROWS, 1024), BF16),
            pltpu.VMEM((ROWS, 256), BF16),
            dma((3,)),
            dma((6, 2)),
            dma((6, 2)),
            dma((5, 2)),
            dma((5, 2)),
            dma(()),
            dma(()),
            dma(()),
            dma(()),
            dma(()),
            dma(()),
            dma(()),
            dma(()),
            dma((2,)),
        ],
        compiler_params=pltpu.CompilerParams(
            collective_id=0, has_side_effects=True, vmem_limit_bytes=56 * 1024 * 1024
        ),
    )(thermal, deform, modulus, plastic, flag, holder, position)


def decode_kernel(words, plastic, exponents, heat_out, moved_out, plastic_out):
    scales = [jnp.exp2(exponents[:, f : f + 1]) * (1.0 / (32767.0 * 32767.0)) for f in range(4)]

    def piece(m, carry):
        at = pl.ds(pl.multiple_of(128 * m, 128), 128)
        for w in range(2):
            word = words[m, 16 * w : 16 * w + 16, :]
            for part in range(2):
                code = lax.shift_right_logical(word, 16) if part == 0 else word & 65535
                root = (code - 32768).astype(F32)
                field = root * jnp.abs(root) * scales[2 * w + part]
                if w == 0 and part == 0:
                    heat_out[0, 0, :, at] = field
                else:
                    moved_out[0, 0, :, 2 * w + part - 1, at] = field
        word = plastic[m]
        for part in range(2):
            code = lax.shift_right_logical(word, 16) if part == 0 else word & 65535
            root = code.astype(F32) * (1.0 / PLASTIC_STEPS) + PLASTIC_LOW
            plastic_out[0, 0, 8 * part : 8 * part + 8, at] = root * root
        return carry

    lax.fori_loop(0, N_SLAB, piece, 0)


def decode(words, plastic, exponents):
    vmem = pl.BlockSpec(memory_space=pltpu.VMEM)
    length = EDGE**3
    return pl.pallas_call(
        decode_kernel,
        name="decode",
        out_shape=(
            jax.ShapeDtypeStruct((1, 1, P_DEV, length), F32),
            jax.ShapeDtypeStruct((1, 1, P_DEV, 3, length), F32),
            jax.ShapeDtypeStruct((1, 1, P_DEV, length), F32),
        ),
        in_specs=[vmem] * 3,
        out_specs=(vmem,) * 3,
        compiler_params=pltpu.CompilerParams(vmem_limit_bytes=24 * 1024 * 1024),
    )(words, plastic, exponents)


def on_device(thermal, deform, modulus, plastic, flag, holder, position):
    return decode(*move(thermal, deform, modulus, plastic, flag, holder, position))


def solution(mesh):
    placed = (
        P("slab", "blk", None),
        P(None, "slab", "blk", None),
        P("slab", "blk", None),
        P("slab", "blk", None),
        P("slab", "blk", None),
        P("slab", "blk", None),
        P("slab", "blk", None),
    )
    return jax.shard_map(
        on_device,
        mesh=mesh,
        in_specs=placed,
        out_specs=(
            P("slab", "blk", None, None),
            P("slab", "blk", None, None, None),
            P("slab", "blk", None, None),
        ),
        check_vma=False,
    )
```

time: 702 us -> 77.9 us (0.11)
  the two profiles are of different devices: /device:TPU:36 before, /device:TPU:1 now
where the time goes in v1:
time: 77.9 us; the launch traced here: 77.7 us
  Pallas kernels  73 us (94%)
  local copies, waits for them, and re-layouts  3.97 us (5%)
    pallas_call x1, Pallas kernels, move(): pl.pallas_call(move_kernel, name='sweep_solve_move', out_shape=(jax.Shape...  69.5 us
    pallas_call x1, Pallas kernels, decode(): pl.pallas_call(decode_kernel, name='decode', out_shape=(jax.ShapeDtypeStr...  3.55 us
    unnamed x6, local copies, waits for them, and re-layouts  2.63 us

profile of v1, /device:TPU:1, one launch (start us, length us, event | category | flops | bytes accessed | tf_op | source)
XLA Modules:
  0.0 77.7 jit_solution(177090653052944737)
XLA Ops:
  0.6 69.5 %sweep_solve_move.1 = (s32[32,32,128]{2,1,0:T(8,128)}, s32[32,8,128]{2,1,0:T(8,128)}, f32[16,128]{1,0:T(8,128)}) custom-call(f32[16,16,256]{2,1,0:T(8,128)} %thermal.1, f32[3,16,16,256]{3,2,1,0:T(8,128)} %deform.1, f32[16,16,256]{2,1,0:T(8,128)} %modulus.1, f32[16,16,256]{2,1,0:T(8,128)} %plastic.1, s32[1,1,16]{2,1,0:T(1,128)} %flag.1, s32[1,1,16]{2,1,0:T(1,128)} %holder.1, ...), custom_call_target="tpu_custom_call" | custom-call | tf_op jit(solution)/shard_map/sweep_solve_move/pallas_call | solution.py:556
  70.1 0.0 copy-start
  70.1 1.0 %copy-done = s32[32,32,128]{2,1,0:T(8,128)S(1)} copy-done((s32[32,32,128]{2,1,0:T(8,128)S(1)}, s32[32,32,128]{2,1,0:T(8,128)}, u32[]{:S(2)}) %copy-start) | copy-done | bytes 524312
  71.2 0.0 copy-start.1
  71.2 0.9 %copy-done.1 = s32[32,8,128]{2,1,0:T(8,128)S(1)} copy-done((s32[32,8,128]{2,1,0:T(8,128)S(1)}, s32[32,8,128]{2,1,0:T(8,128)}, u32[]{:S(2)}) %copy-start.1) | copy-done | bytes 131096
  72.1 0.0 copy-start.2
  72.1 0.7 copy-done.2
  72.8 3.6 %decode.1 = (f32[1,1,16,4096]{3,2,1,0:T(8,128)}, f32[1,1,16,3,4096]{4,3,2,1,0:T(4,128)S(1)}, f32[1,1,16,4096]{3,2,1,0:T(8,128)}) custom-call(s32[32,32,128]{2,1,0:T(8,128)S(1)} %copy-done, s32[32,8,128]{2,1,0:T(8,128)S(1)} %copy-done.1, f32[16,128]{1,0:T(8,128)S(1)} %copy-done.2), custom_call_target="tpu_custom_call" | custom-call | tf_op jit(solution)/shard_map/decode/pallas_call | solution.py:642
  76.3 1.3 %copy.10 = f32[1,1,16,3,4096]{4,2,3,1,0:T(8,128)} copy(f32[1,1,16,3,4096]{4,3,2,1,0:T(4,128)S(1)} %get-tuple-element.10) | data formatting | bytes 1572864 | tf_op jit(solution)/shard_map/decode/pallas_call | solution.py:642
Async XLA Ops:
  70.1 1.0 %copy-start = (s32[32,32,128]{2,1,0:T(8,128)S(1)}, s32[32,32,128]{2,1,0:T(8,128)}, u32[]{:S(2)}) copy-start(s32[32,32,128]{2,1,0:T(8,128)} %get-tuple-element.6.words) | copy-start | bytes 1572868
  71.2 0.9 %copy-start.1 = (s32[32,8,128]{2,1,0:T(8,128)S(1)}, s32[32,8,128]{2,1,0:T(8,128)}, u32[]{:S(2)}) copy-start(s32[32,8,128]{2,1,0:T(8,128)} %get-tuple-element.7.plastic) | copy-start | bytes 393220
  72.1 0.7 copy-start.2

commit v2 on v1

--- a/solution.py
+++ b/solution.py
@@ -42,23 +42,33 @@
     return lax.broadcasted_iota(I32, shape, 0)
 
 
-def shifted_planes(plane, row, inner):
-    below = jnp.where(inner == 0, 0.0, pltpu.roll(plane, 1, 1))
-    above = jnp.where(inner == EDGE - 1, 0.0, pltpu.roll(plane, DEPTH - 1, 1))
-    three = (below, plane, above)
-    low = [jnp.where(row == 0, 0.0, pltpu.roll(part, 1, 0)) for part in three]
-    high = [jnp.where(row == EDGE - 1, 0.0, pltpu.roll(part, EDGE - 1, 0)) for part in three]
-    return low + list(three) + high
-
-
-def swap_rows_and_groups(tile, row, group):
+def shifted_pairs(pair, row8):
+    low, high = pair
+    out = [None] * 9
+    for dz in (-1, 0, 1):
+        a, b = (low, high) if dz == 0 else [pltpu.roll(part, 1 if dz < 0 else 127, 1) for part in pair]
+        a_down, b_down = pltpu.roll(a, 1, 0), pltpu.roll(b, 1, 0)
+        a_up, b_up = pltpu.roll(a, 7, 0), pltpu.roll(b, 7, 0)
+        out[plane_number(-1, dz)] = (a_down, jnp.where(row8 == 0, a_down, b_down))
+        out[plane_number(0, dz)] = (a, b)
+        out[plane_number(1, dz)] = (jnp.where(row8 == 7, b_up, a_up), b_up)
+    return out
+
+
+def swap_rows_and_groups(tiles, group, first, second):
+    for k in range(8):
+        first[8 * k : 8 * k + 8, :] = tiles[k]
+    parts = [first[pl.ds(k, 8, stride=8), :] for k in range(8)]
     for bit in (4, 2, 1):
-        row_bit = (row & bit) != 0
-        group_bit = (group & bit) != 0
-        down = pltpu.roll(pltpu.roll(tile, bit, 0), 128 - 16 * bit, 1)
-        up = down if bit == 4 else pltpu.roll(pltpu.roll(tile, 8 - bit, 0), 16 * bit, 1)
-        tile = jnp.where(row_bit == group_bit, tile, jnp.where(row_bit, down, up))
-    return tile
+        low_group = (group & bit) == 0
+        for k in range(8):
+            if k & bit == 0:
+                low, high = parts[k], parts[k | bit]
+                parts[k] = jnp.where(low_group, low, pltpu.roll(high, 16 * bit, 1))
+                parts[k | bit] = jnp.where(low_group, pltpu.roll(low, 128 - 16 * bit, 1), high)
+    for k in range(8):
+        second[8 * k : 8 * k + 8, :] = parts[k]
+    return [second[pl.ds(k, 8, stride=8), :] for k in range(8)]
 
 
 def byte_of(words, number):
@@ -77,12 +87,13 @@
     face_x, face_ym, face_yp, face_zm, face_zp, centre,
     stiff, weights, tile, inverse, values,
     send_one, recv_one, send_two, plastic_one, plastic_got, plastic_two,
-    one_hot, table, plastic_table,
+    one_hot, table, plastic_table, swap_a, swap_b,
     load_sem, x_send, x_recv, y_send, y_recv,
     one_send, one_recv, two_send, two_recv, pl_one_send, pl_one_recv, pl_two_send, pl_two_recv, own_sem,
 ):
     s = lax.axis_index("slab")
     b = lax.axis_index("blk")
+    chip = s // 2
     up, down = lax.rem(s + 1, N_SLAB), lax.rem(s + N_SLAB - 1, N_SLAB)
     right, left = lax.rem(b + 1, N_BLK), lax.rem(b + N_BLK - 1, N_BLK)
     has_up, has_down = s < N_SLAB - 1, s > 0
@@ -227,31 +238,44 @@
         code = holder[0, 0, p] * P_DEV + position[0, 0, p]
         slot_row = jnp.where(slot_lane == lax.rem(s, 8) * P_DEV + p, code, slot_row)
 
+    sibling = lax.bitwise_xor(s, 1)
+
+    def send_plastic(m):
+        pltpu.make_async_remote_copy(
+            plastic_one.at[m, pl.ds(0, 9)], plastic_got.at[s, pl.ds(0, 9)], pl_one_send, pl_one_recv,
+            device_id=(m, b), device_id_type=MESH,
+        ).start()
+
+    def plastic_planes(planes):
+        tiles = []
+        for x in planes:
+            root = plastic[x]
+            root = root * lax.rsqrt(root)
+            codes = jnp.clip((root - PLASTIC_LOW) * PLASTIC_STEPS + 0.5, 0.0, 65535.0).astype(I32)
+            words = (codes[:, 0:128] << 16) | codes[:, 128:256]
+            tiles += [words[0:8], words[8:16]]
+        tiles = swap_rows_and_groups(tiles, group8, swap_a, swap_b)
+        for k in range(8):
+            m = 2 * planes[k // 2] + k % 2
+            plastic_one[m, 0:8, :] = tiles[k]
+            plastic_one[m, 8:9, :] = slot_row
+
     def plastic_out(step, carry):
-        x = lax.rem(step + s // 2, EDGE)
-        root = plastic[x]
-        root = root * lax.rsqrt(root)
-        codes = jnp.clip((root - PLASTIC_LOW) * PLASTIC_STEPS + 0.5, 0.0, 65535.0).astype(I32)
-        words = (codes[:, 0:128] << 16) | codes[:, 128:256]
-        for half in range(2):
-            m = 2 * x + half
-            plastic_one[m, 0:8, :] = swap_rows_and_groups(words[8 * half : 8 * half + 8], row8, group8)
-            plastic_one[m, 8:9, :] = slot_row
-
-            @pl.when(m != s)
-            def _():
-                pltpu.make_async_remote_copy(
-                    plastic_one.at[m, pl.ds(0, 9)], plastic_got.at[s, pl.ds(0, 9)], pl_one_send, pl_one_recv,
-                    device_id=(m, b), device_id_type=MESH,
-                ).start()
-
-            @pl.when(m == s)
-            def _():
-                plastic_got[s, 0:9, :] = plastic_one[m, 0:9, :]
-
-        return carry
-
-    lax.fori_loop(0, EDGE, plastic_out, 0)
+        planes = [lax.rem(chip + 4 * step + j, EDGE) for j in range(4)]
+        plastic_planes(planes)
+        for x in planes:
+            send_plastic(2 * x)
+            send_plastic(2 * x + 1)
+        return carry
+
+    planes = [lax.rem(chip + j, EDGE) for j in range(4)]
+    plastic_planes(planes)
+    send_plastic(sibling)
+    plastic_got[s, 0:9, :] = plastic_one[s, 0:9, :]
+    for x in planes[1:]:
+        send_plastic(2 * x)
+        send_plastic(2 * x + 1)
+    lax.fori_loop(1, 4, plastic_out, 0)
 
     for dy in (-1, 0, 1):
         for dz in (-1, 0, 1):
@@ -260,11 +284,12 @@
             weights[0, plane_number(dy, dz)] = jnp.where(inside, 0.5 * WEIGHTS[reach], 0.0)
             weights[1, plane_number(dy, dz)] = jnp.where(inside, 0.5 * WEIGHTS[reach + 1], 0.0)
     for n in range(9):
-        for place in (0, EDGE + 1):
-            stiff[n, place] = zero_plane
-            for k in range(2):
-                for f in range(4):
-                    values[k, f, n, place] = zero_plane
+        for f in range(4):
+            values[f, n, 0] = zero_plane
+            values[f, n, EDGE + 1] = zero_plane
+    for number, (dx, dy, dz) in enumerate(OFFSETS):
+        if dx != 0:
+            tile[number, 1 if dx < 0 else EDGE] = zero_plane
 
     factor = jnp.ones((1, DEPTH), F32)
     lane_row = lane_of((1, DEPTH)) // EDGE
@@ -370,29 +395,30 @@
 
     lax.fori_loop(0, 8, plastic_unpack, 0)
 
-    def plastic_on(step, carry):
-        g = lax.rem(step + s // 8, 4)
+    def plastic_group(g):
         place = pl.ds(pl.multiple_of(128 * g, 128), 128)
         rows = jnp.dot(one_hot[place, :], plastic_table[...], preferred_element_type=F32)
         codes = joined(rows[:, 0:128], rows[:, 128:256]).reshape(8, P_DEV, 128)
         plastic_two[pl.ds(8 * g, 8)] = (codes[:, 0:8] << 16) | codes[:, 8:16]
+
+    def pass_plastic(d):
+        pltpu.make_async_remote_copy(
+            plastic_two.at[d], out_plastic.at[s], pl_two_send, pl_two_recv,
+            device_id=(d, b), device_id_type=MESH,
+        ).start()
+
+    def plastic_on(step, carry):
+        g = lax.rem(step + s // 8, 4)
+        plastic_group(g)
         for k in range(8):
-            d = 8 * g + lax.rem(s + k, 8)
-
-            @pl.when(d != s)
-            def _():
-                pltpu.make_async_remote_copy(
-                    plastic_two.at[d], out_plastic.at[s], pl_two_send, pl_two_recv,
-                    device_id=(d, b), device_id_type=MESH,
-                ).start()
-
-            @pl.when(d == s)
-            def _():
-                pltpu.make_async_copy(plastic_two.at[d], out_plastic.at[s], own_sem.at[0]).start()
-
-        return carry
-
-    lax.fori_loop(0, 4, plastic_on, 0)
+            pass_plastic(8 * g + lax.rem(s + k, 8))
+        return carry
+
+    plastic_group(s // 8)
+    pltpu.make_async_copy(plastic_two.at[s], out_plastic.at[s], own_sem.at[0]).start()
+    for k in range(1, 8):
+        pass_plastic(8 * (s // 8) + lax.rem(s + k, 8))
+    lax.fori_loop(1, 4, plastic_on, 0)
 
     for t in range(1, SWEEPS):
         wait_recv(x_copies(t), has_up, has_down)
@@ -402,12 +428,7 @@
     def prepare(x, most):
         fields = [state[SWEEPS, f, x + 1] for f in range(4)]
         squared = fields[0] * fields[0]
-        stiffness = cond[x + 1] * (1.0 + 0.5 * squared / (1.0 + squared)) / (1.0 + plastic[x]) * factor
-        for n, plane in enumerate(shifted_planes(stiffness, row, inner)):
-            stiff[n, x + 1] = plane
-        for f in range(4):
-            for n, plane in enumerate(shifted_planes(fields[f], row, inner)):
-                values[0, f, n, x + 1] = plane
+        stiff[x + 1] = cond[x + 1] * (1.0 + 0.5 * squared / (1.0 + squared)) / (1.0 + plastic[x]) * factor
         return tuple(jnp.maximum(most[f], jnp.abs(fields[f])) for f in range(4))
 
     most = lax.fori_loop(0, EDGE, prepare, (zero_plane,) * 4)
@@ -420,74 +441,111 @@
         scales.append(jnp.exp2(-exponent))
         exponent_row = jnp.where(slot_lane == f, exponent.astype(I32), exponent_row)
 
-    def build(x, carry):
-        own = stiff[4, x + 1]
-        total = jnp.ones((EDGE, DEPTH), F32)
-        for number, (dx, dy, dz) in enumerate(OFFSETS):
-            n = plane_number(dy, dz)
-            weight = weights[abs(dx), n]
-            entry = weight * (own + stiff[n, x + 1 + dx])
-            if dx < 0:
-                entry = entry * (x > 0).astype(F32)
-            if dx > 0:
-                entry = entry * (x < EDGE - 1).astype(F32)
-            entry = entry.astype(BF16).astype(F32)
-            tile[number, x] = entry
-            total = total + entry
-        inverse[x] = 1.0 / total
-        return carry
-
-    lax.fori_loop(0, EDGE, build, 0)
-
-    def smoothed(k, x):
+    numbers = {offset: number for number, offset in enumerate(OFFSETS)}
+    halves = (slice(0, 8), slice(8, 16))
+    ones = (jnp.ones((8, 128), F32),) * 2
+
+    def built(x, done, active, side):
+        lanes = slice(128 * side, 128 * side + 128)
+        begun = [ones] + [tuple(state[SWEEPS, f, x + 2, rows, lanes] for rows in halves) for f in range(4)]
+        totals = {1: list(done), 0: list(active), -1: begun}
+        own = {dx: [stiff[x + 1 - dx, rows, lanes] for rows in halves] for dx in (-1, 0, 1)}
+        near = shifted_pairs(own[0], row8)
+        fields = [
+            shifted_pairs([state[SWEEPS, f, x + 1, rows, lanes] for rows in halves], row8) for f in range(4)
+        ]
+        for dz in (-1, 0, 1):
+            for dy in (-1, 0, 1):
+                n = plane_number(dy, dz)
+                for dx in (-1, 0, 1):
+                    if (dx, dy, dz) == (0, 0, 0):
+                        continue
+                    number = numbers[dx, dy, dz]
+                    entries = []
+                    for j, rows in enumerate(halves):
+                        entry = weights[abs(dx), n, rows, 0:128] * (own[dx][j] + near[n][j])
+                        entry = entry.astype(BF16).astype(F32)
+                        tile[number, x + 1 - dx, rows, lanes] = entry
+                        entries.append(entry)
+                    total = totals[dx]
+                    total[0] = tuple(total[0][j] + entries[j] for j in range(2))
+                    for f in range(4):
+                        total[f + 1] = tuple(total[f + 1][j] + entries[j] * fields[f][n][j] for j in range(2))
+        return tuple(totals[1]), tuple(totals[0]), tuple(totals[-1])
+
+    def finish(place, done, side):
+        lanes = slice(128 * side, 128 * side + 128)
+        scale = [1.0 / part for part in done[0]]
+        for j, rows in enumerate(halves):
+            inverse[place, rows, lanes] = scale[j]
+        for f in range(4):
+            field = [done[f + 1][j] * scale[j] for j in range(2)]
+            for n, pair in enumerate(shifted_pairs(field, row8)):
+                for j, rows in enumerate(halves):
+                    values[f, n, place, rows, lanes] = pair[j]
+
+    for side in range(2):
+
+        def source(x, carry):
+            done, active, begun = built(x, *carry, side)
+
+            @pl.when(x > 0)
+            def _():
+                finish(x, done, side)
+
+            return active, begun
+
+        lanes = slice(128 * side, 128 * side + 128)
+        start_at = (ones,) + tuple(tuple(state[SWEEPS, f, 1, rows, lanes] for rows in halves) for f in range(4))
+        last, _ = lax.fori_loop(0, EDGE, source, ((ones,) * 5, start_at))
+        finish(EDGE, last, side)
+
+    def smoothed(x):
         totals = [state[SWEEPS, f, x + 1] for f in range(4)]
         for number, (dx, dy, dz) in enumerate(OFFSETS):
-            entry = tile[number, x]
+            entry = tile[number, x + 1]
             for f in range(4):
-                totals[f] = totals[f] + entry * values[k, f, plane_number(dy, dz), x + 1 + dx]
-        scale = inverse[x]
+                totals[f] = totals[f] + entry * values[f, plane_number(dy, dz), x + 1 + dx]
+        scale = inverse[x + 1]
         return [total * scale for total in totals]
 
-    def first(x, carry):
-        fields = smoothed(0, x)
-        for f in range(4):
-            for n, plane in enumerate(shifted_planes(fields[f], row, inner)):
-                values[1, f, n, x + 1] = plane
-        return carry
-
-    lax.fori_loop(0, EDGE, first, 0)
-
-    def second(step, carry):
-        x = lax.rem(step + s // 2, EDGE)
+    def send_plane(m):
+        pltpu.make_async_remote_copy(
+            send_one.at[m, pl.ds(0, 33)], recv_one.at[s, pl.ds(0, 33)], one_send, one_recv,
+            device_id=(m, b), device_id_type=MESH,
+        ).start()
+
+    def second_plane(x):
         codes = []
-        for f, field in enumerate(smoothed(1, x)):
+        for f, field in enumerate(smoothed(x)):
             part = jnp.abs(field) * scales[f]
             part = jnp.minimum(part * lax.rsqrt(part + 1e-37), 1.0) * 32767.0
             codes.append((jnp.where(field < 0.0, -part, part) + 32768.5).astype(I32))
         words = [(codes[0] << 16) | codes[1], (codes[2] << 16) | codes[3]]
+        tiles = [
+            words[w][8 * half : 8 * half + 8, 128 * side : 128 * side + 128]
+            for half in range(2)
+            for w in range(2)
+            for side in range(2)
+        ]
+        tiles = swap_rows_and_groups(tiles, group8, swap_a, swap_b)
         for half in range(2):
             m = 2 * x + half
-            for w in range(2):
-                for side in range(2):
-                    part = words[w][8 * half : 8 * half + 8, 128 * side : 128 * side + 128]
-                    place = 16 * w + 8 * side
-                    send_one[m, place : place + 8, :] = swap_rows_and_groups(part, row8, group8)
+            for k in range(4):
+                send_one[m, 8 * k : 8 * k + 8, :] = tiles[4 * half + k]
             send_one[m, 32:33, :] = exponent_row
 
-            @pl.when(m != s)
-            def _():
-                pltpu.make_async_remote_copy(
-                    send_one.at[m, pl.ds(0, 33)], recv_one.at[s, pl.ds(0, 33)], one_send, one_recv,
-                    device_id=(m, b), device_id_type=MESH,
-                ).start()
-
-            @pl.when(m == s)
-            def _():
-                recv_one[s, 0:33, :] = send_one[m, 0:33, :]
-
-        return carry
-
-    lax.fori_loop(0, EDGE, second, 0)
+    def second(step, carry):
+        x = lax.rem(step + chip, EDGE)
+        second_plane(x)
+        send_plane(2 * x)
+        send_plane(2 * x + 1)
+        return carry
+
+    second_plane(chip)
+    send_plane(sibling)
+    recv_one[s, 0:33, :] = send_one[s, 0:33, :]
+    lax.fori_loop(1, EDGE, second, 0)
     wait_all(recv_one.at[pl.ds(0, N_SLAB - 1), pl.ds(0, 33)], one_recv)
 
     def unpack(g, carry):
@@ -501,31 +559,32 @@
 
     lax.fori_loop(0, 8, unpack, 0)
 
-    def onward(step, carry):
-        g = lax.rem(step + s // 8, 4)
+    def onward_group(g):
         place = pl.ds(pl.multiple_of(128 * g, 128), 128)
         rows = jnp.dot(one_hot[place, :], table[...], preferred_element_type=F32)
         for w in range(2):
             parts = [rows[:, 128 * (4 * w + n) : 128 * (4 * w + n) + 128] for n in range(4)]
             words = joined(parts[0], parts[1]) | (joined(parts[2], parts[3]) << 16)
             send_two[pl.ds(8 * g, 8), 16 * w : 16 * w + 16, :] = words.reshape(8, P_DEV, 128)
+
+    def pass_on(d):
+        pltpu.make_async_remote_copy(
+            send_two.at[d], out_words.at[s], two_send, two_recv,
+            device_id=(d, b), device_id_type=MESH,
+        ).start()
+
+    def onward(step, carry):
+        g = lax.rem(step + s // 8, 4)
+        onward_group(g)
         for k in range(8):
-            d = 8 * g + lax.rem(s + k, 8)
-
-            @pl.when(d != s)
-            def _():
-                pltpu.make_async_remote_copy(
-                    send_two.at[d], out_words.at[s], two_send, two_recv,
-                    device_id=(d, b), device_id_type=MESH,
-                ).start()
-
-            @pl.when(d == s)
-            def _():
-                pltpu.make_async_copy(send_two.at[d], out_words.at[s], own_sem.at[1]).start()
-
-        return carry
-
-    lax.fori_loop(0, 4, onward, 0)
+            pass_on(8 * g + lax.rem(s + k, 8))
+        return carry
+
+    onward_group(s // 8)
+    pltpu.make_async_copy(send_two.at[s], out_words.at[s], own_sem.at[1]).start()
+    for k in range(1, 8):
+        pass_on(8 * (s // 8) + lax.rem(s + k, 8))
+    lax.fori_loop(1, 4, onward, 0)
 
     sources = jnp.concatenate(
         [jnp.broadcast_to(recv_one[k, 32:33, :].astype(F32), (P_DEV, 128)) for k in range(N_SLAB)], axis=0
@@ -576,11 +635,11 @@
             pltpu.VMEM((EDGE,) + plane, F32),
             pltpu.VMEM((EDGE,) + plane, F32),
             pltpu.VMEM((EDGE,) + plane, F32),
-            pltpu.VMEM((9, EDGE + 2) + plane, F32),
+            pltpu.VMEM((EDGE + 2,) + plane, F32),
             pltpu.VMEM((2, 9) + plane, F32),
-            pltpu.VMEM((26, EDGE) + plane, F32),
-            pltpu.VMEM((EDGE,) + plane, F32),
-            pltpu.VMEM((2, 4, 9, EDGE + 2) + plane, F32),
+            pltpu.VMEM((26, EDGE + 2) + plane, F32),
+            pltpu.VMEM((EDGE + 1,) + plane, F32),
+            pltpu.VMEM((4, 9, EDGE + 2) + plane, F32),
             pltpu.VMEM((N_SLAB, 40, 128), I32),
             pltpu.VMEM((N_SLAB, 40, 128), I32),
             pltpu.VMEM((N_SLAB, 32, 128), I32),
@@ -590,6 +649,8 @@
             pltpu.VMEM((ROWS, ROWS), BF16),
             pltpu.VMEM((ROWS, 1024), BF16),
             pltpu.VMEM((ROWS, 256), BF16),
+            pltpu.VMEM((64, 128), I32),
+            pltpu.VMEM((64, 128), I32),
             dma((3,)),
             dma((6, 2)),
             dma((6, 2)),
@@ -611,46 +672,82 @@
     )(thermal, deform, modulus, plastic, flag, holder, position)
 
 
-def decode_kernel(words, plastic, exponents, heat_out, moved_out, plastic_out):
-    scales = [jnp.exp2(exponents[:, f : f + 1]) * (1.0 / (32767.0 * 32767.0)) for f in range(4)]
-
-    def piece(m, carry):
-        at = pl.ds(pl.multiple_of(128 * m, 128), 128)
-        for w in range(2):
-            word = words[m, 16 * w : 16 * w + 16, :]
+def decode_kernel(
+    words_in, plastic_in, exponents, heat_out, moved_out, plastic_out, words, strain, heat, moved, straight, got, put
+):
+    pieces = N_SLAB // 4
+    fetch = [
+        pltpu.make_async_copy(words_in.at[pl.ds(pieces * k, pieces)], words.at[pl.ds(pieces * k, pieces)], got.at[k])
+        for k in range(4)
+    ]
+    fetch.append(pltpu.make_async_copy(plastic_in, strain, got.at[4]))
+    for copy in fetch:
+        copy.start()
+    scales = [
+        jnp.broadcast_to(jnp.exp2(exponents[:, f : f + 1]) * (1.0 / (32767.0 * 32767.0)), (P_DEV, 128))
+        for f in range(4)
+    ]
+    length = 128 * pieces
+    writes = []
+    for k in range(4):
+        fetch[k].wait()
+        for m in range(pieces * k, pieces * k + pieces):
+            at = slice(128 * m, 128 * m + 128)
+            for w in range(2):
+                word = words[m, 16 * w : 16 * w + 16, :]
+                for part in range(2):
+                    code = lax.shift_right_logical(word, 16) if part == 0 else word & 65535
+                    root = (code - 32768).astype(F32)
+                    field = root * jnp.abs(root) * scales[2 * w + part]
+                    if w == 0 and part == 0:
+                        heat[:, at] = field
+                    else:
+                        moved[2 * w + part - 1, :, at] = field
+        at = pl.ds(length * k, length)
+        writes.append(pltpu.make_async_copy(heat.at[:, at], heat_out.at[0, 0, :, at], put.at[3 * k]))
+        writes.append(pltpu.make_async_copy(moved.at[:, :, at], moved_out.at[0, 0, :, :, at], put.at[3 * k + 1]))
+        for copy in writes[-2:]:
+            copy.start()
+        if k == 0:
+            fetch[4].wait()
+        for m in range(pieces * k, pieces * k + pieces):
+            word = strain[m]
             for part in range(2):
                 code = lax.shift_right_logical(word, 16) if part == 0 else word & 65535
-                root = (code - 32768).astype(F32)
-                field = root * jnp.abs(root) * scales[2 * w + part]
-                if w == 0 and part == 0:
-                    heat_out[0, 0, :, at] = field
-                else:
-                    moved_out[0, 0, :, 2 * w + part - 1, at] = field
-        word = plastic[m]
-        for part in range(2):
-            code = lax.shift_right_logical(word, 16) if part == 0 else word & 65535
-            root = code.astype(F32) * (1.0 / PLASTIC_STEPS) + PLASTIC_LOW
-            plastic_out[0, 0, 8 * part : 8 * part + 8, at] = root * root
-        return carry
-
-    lax.fori_loop(0, N_SLAB, piece, 0)
+                root = code.astype(F32) * (1.0 / PLASTIC_STEPS) + PLASTIC_LOW
+                straight[8 * part : 8 * part + 8, 128 * m : 128 * m + 128] = root * root
+        writes.append(pltpu.make_async_copy(straight.at[:, at], plastic_out.at[0, 0, :, at], put.at[3 * k + 2]))
+        writes[-1].start()
+    for copy in writes:
+        copy.wait()
 
 
 def decode(words, plastic, exponents):
     vmem = pl.BlockSpec(memory_space=pltpu.VMEM)
+    anywhere = pl.BlockSpec(memory_space=pl.ANY)
     length = EDGE**3
-    return pl.pallas_call(
+    heat, moved, strain = pl.pallas_call(
         decode_kernel,
         name="decode",
         out_shape=(
             jax.ShapeDtypeStruct((1, 1, P_DEV, length), F32),
-            jax.ShapeDtypeStruct((1, 1, P_DEV, 3, length), F32),
+            jax.ShapeDtypeStruct((1, 1, 3, P_DEV, length), F32),
             jax.ShapeDtypeStruct((1, 1, P_DEV, length), F32),
         ),
-        in_specs=[vmem] * 3,
-        out_specs=(vmem,) * 3,
-        compiler_params=pltpu.CompilerParams(vmem_limit_bytes=24 * 1024 * 1024),
+        in_specs=[anywhere, anywhere, vmem],
+        out_specs=(anywhere,) * 3,
+        scratch_shapes=[
+            pltpu.VMEM((N_SLAB, 32, 128), I32),
+            pltpu.VMEM((N_SLAB, 8, 128), I32),
+            pltpu.VMEM((P_DEV, length), F32),
+            pltpu.VMEM((3, P_DEV, length), F32),
+            pltpu.VMEM((P_DEV, length), F32),
+            pltpu.SemaphoreType.DMA((5,)),
+            pltpu.SemaphoreType.DMA((12,)),
+        ],
+        compiler_params=pltpu.CompilerParams(vmem_limit_bytes=56 * 1024 * 1024),
     )(words, plastic, exponents)
+    return heat, moved.transpose(0, 1, 3, 2, 4), strain
 
 
 def on_device(thermal, deform, modulus, plastic, flag, holder, position):

time: 77.9 us -> 65.9 us (0.85)
  Pallas kernels: 73 us -> 65.1 us
  local copies, waits for them, and re-layouts: 3.97 us -> 0 us
    pallas_call x1, Pallas kernels: 69.5 us -> 62.1 us  [move(): pl.pallas_call(move_kernel, name='sweep_solve_move', out_shape=(jax.Shape...]
    unnamed x6 -> x0, local copies, waits for them, and re-layouts: 2.63 us -> none
    pallas_call x1 -> x0, local copies, waits for them, and re-layouts: 1.34 us -> none  [decode(): pl.pallas_call(decode_kernel, name='decode', out_shape=(jax.ShapeDtypeStr...]
where the time goes in v2:
time: 65.9 us; the launch traced here: 65.7 us
  Pallas kernels  65.1 us (99%)
    pallas_call x1, Pallas kernels, move(): pl.pallas_call(move_kernel, name='sweep_solve_move', out_shape=(jax.Shape...  62.1 us
    pallas_call x1, Pallas kernels, decode(): pl.pallas_call(decode_kernel, name='decode', out_shape=(jax.ShapeDtypeStr...  2.99 us

profile of v2, /device:TPU:1, one launch (start us, length us, event | category | flops | bytes accessed | tf_op | source)
XLA Modules:
  0.0 65.7 jit_solution(11714783656794844267)
XLA Ops:
  0.6 62.1 %sweep_solve_move.1 = (s32[32,32,128]{2,1,0:T(8,128)}, s32[32,8,128]{2,1,0:T(8,128)}, f32[16,128]{1,0:T(8,128)}) custom-call(f32[16,16,256]{2,1,0:T(8,128)} %thermal.1, f32[3,16,16,256]{3,2,1,0:T(8,128)} %deform.1, f32[16,16,256]{2,1,0:T(8,128)} %modulus.1, f32[16,16,256]{2,1,0:T(8,128)} %plastic.1, s32[1,1,16]{2,1,0:T(1,128)} %flag.1, s32[1,1,16]{2,1,0:T(1,128)} %holder.1, ...), custom_call_target="tpu_custom_call" | custom-call | tf_op jit(solution)/shard_map/sweep_solve_move/pallas_call | solution.py:615
  62.7 3.0 %decode.1 = (f32[1,1,16,4096]{3,2,1,0:T(8,128)}, f32[1,1,3,16,4096]{4,3,2,1,0:T(8,128)}, f32[1,1,16,4096]{3,2,1,0:T(8,128)}) custom-call(s32[32,32,128]{2,1,0:T(8,128)} %get-tuple-element.9.words_in, s32[32,8,128]{2,1,0:T(8,128)} %get-tuple-element.10.plastic_in, f32[16,128]{1,0:T(8,128)} %get-tuple-element.11.exponents), custom_call_target="tpu_custom_call" | custom-call | tf_op jit(solution)/shard_map/decode/pallas_call | solution.py:729

commit v3 on v2

--- a/solution.py
+++ b/solution.py
@@ -42,11 +42,9 @@
     return lax.broadcasted_iota(I32, shape, 0)
 
 
-def shifted_pairs(pair, row8):
-    low, high = pair
+def shifted_pairs(three, row8):
     out = [None] * 9
-    for dz in (-1, 0, 1):
-        a, b = (low, high) if dz == 0 else [pltpu.roll(part, 1 if dz < 0 else 127, 1) for part in pair]
+    for dz, (a, b) in zip((-1, 0, 1), three):
         a_down, b_down = pltpu.roll(a, 1, 0), pltpu.roll(b, 1, 0)
         a_up, b_up = pltpu.roll(a, 7, 0), pltpu.roll(b, 7, 0)
         out[plane_number(-1, dz)] = (a_down, jnp.where(row8 == 0, a_down, b_down))
@@ -81,11 +79,11 @@
 
 
 def move_kernel(
-    thermal, deform, modulus, plastic, flag, holder, position,
+    thermal, deform, modulus, plastic_in, flag, holder, position,
     out_words, out_plastic, out_exponents,
-    state, halo_y, stage_y, cond, cond_y, cond_stage,
+    plastic, state, halo_y, stage_y, cond, cond_y, cond_stage,
     face_x, face_ym, face_yp, face_zm, face_zp, centre,
-    stiff, weights, tile, inverse, values,
+    stiff, turned, stepped, coded, weights, tile, inverse, values,
     send_one, recv_one, send_two, plastic_one, plastic_got, plastic_two,
     one_hot, table, plastic_table, swap_a, swap_b,
     load_sem, x_send, x_recv, y_send, y_recv,
@@ -99,30 +97,28 @@
     has_up, has_down = s < N_SLAB - 1, s > 0
     has_right, has_left = b < N_BLK - 1, b > 0
 
+    barrier = pltpu.get_barrier_semaphore()
+
+    for step in range(1, N_SLAB):
+        peer = lax.rem(s + step, N_SLAB)
+        pl.semaphore_signal(barrier, inc=1, device_id=(peer, b), device_id_type=MESH)
+
+    @pl.when(has_right)
+    def _():
+        pl.semaphore_signal(barrier, inc=1, device_id=(s, right), device_id_type=MESH)
+
+    @pl.when(has_left)
+    def _():
+        pl.semaphore_signal(barrier, inc=1, device_id=(s, left), device_id_type=MESH)
+
     loads = [
         pltpu.make_async_copy(thermal, state.at[0, 0, pl.ds(1, EDGE)], load_sem.at[0]),
         pltpu.make_async_copy(deform, state.at[0, pl.ds(1, 3), pl.ds(1, EDGE)], load_sem.at[1]),
         pltpu.make_async_copy(modulus, cond.at[pl.ds(1, EDGE)], load_sem.at[2]),
+        pltpu.make_async_copy(plastic_in, plastic, load_sem.at[3]),
     ]
     for load in loads:
         load.start()
-
-    barrier = pltpu.get_barrier_semaphore()
-
-    def greet(step, carry):
-        peer = lax.rem(s + step, N_SLAB)
-        pl.semaphore_signal(barrier, inc=1, device_id=(peer, b), device_id_type=MESH)
-        return carry
-
-    lax.fori_loop(1, N_SLAB, greet, 0)
-
-    @pl.when(has_right)
-    def _():
-        pl.semaphore_signal(barrier, inc=1, device_id=(s, right), device_id_type=MESH)
-
-    @pl.when(has_left)
-    def _():
-        pl.semaphore_signal(barrier, inc=1, device_id=(s, left), device_id_type=MESH)
 
     zero_plane = jnp.zeros((EDGE, DEPTH), F32)
 
@@ -173,8 +169,12 @@
         for direction, peer in ((0, left), (1, right)):
             if kind == 4:
                 source, target = cond_stage.at[direction], cond_y.at[1 - direction]
+            elif kind == 0:
+                source, target = stage_y.at[0, direction], halo_y.at[0, 1 - direction]
             else:
-                source, target = stage_y.at[kind, direction], halo_y.at[kind, 1 - direction]
+                part = pl.ds(8 * (kind // 4), 8)
+                source = stage_y.at[kind % 4, direction, :, part]
+                target = halo_y.at[kind % 4, 1 - direction, :, part]
             out.append(
                 pltpu.make_async_remote_copy(
                     source, target, y_send.at[kind, direction], y_recv.at[kind, direction],
@@ -200,6 +200,14 @@
         @pl.when(from_low)
         def _():
             copies[1].wait_recv()
+
+    def four_at_a_time(work):
+        def step(k, carry):
+            for j in range(4):
+                work(4 * k + j)
+            return carry
+
+        lax.fori_loop(0, EDGE // 4, step, 0)
 
     def wait_send(copies, to_low, to_high):
         @pl.when(to_low)
@@ -299,7 +307,7 @@
     wait_recv(x_copies(5), has_up, has_down)
     wait_recv(y_copies(4), has_right, has_left)
 
-    def face(x, carry):
+    def face(x):
         here = cond[x + 1]
         ym = jnp.where(row == 0, cond_y[0, pl.ds(x, 1), :], pltpu.roll(here, 1, 0))
         yp = jnp.where(row == EDGE - 1, cond_y[1, pl.ds(x, 1), :], pltpu.roll(here, EDGE - 1, 0))
@@ -315,9 +323,8 @@
         face_zm[x] = zm
         face_zp[x] = zp
         centre[x] = 1.0 - (low + high + ym + yp + zm + zp)
-        return carry
-
-    lax.fori_loop(0, EDGE, face, 0)
+
+    four_at_a_time(face)
 
     def sweep_plane(t, x):
         around = []
@@ -356,18 +363,46 @@
                 stage_y[t + 1, 1, f, pl.ds(x, 1), :] = fresh[f][EDGE - 1 : EDGE]
 
     def sweep(t):
-        def middle(x, carry):
-            sweep_plane(t, x)
-            return carry
-
-        if t + 1 < SWEEPS:
-            sweep_plane(t, 0)
-            sweep_plane(t, EDGE - 1)
-            start(x_copies(t + 1), has_down, has_up)
-            lax.fori_loop(1, EDGE - 1, middle, 0)
+        def four(first):
+            for x in range(first, first + 4):
+                sweep_plane(t, x)
+
+        onward_x = x_copies(t + 1) if t + 1 < SWEEPS else None
+        if t > 0:
+            arrived = x_copies(t)
+
+            @pl.when(has_down)
+            def _():
+                arrived[1].wait_recv()
+
+            wait_recv(y_copies(t), has_right, has_left)
+        four(0)
+        if onward_x:
+
+            @pl.when(has_down)
+            def _():
+                onward_x[0].start()
+
+        four(4)
+        if onward_x:
             start(y_copies(t + 1), has_left, has_right)
-        else:
-            lax.fori_loop(0, EDGE, middle, 0)
+        if t > 0:
+
+            @pl.when(has_up)
+            def _():
+                arrived[0].wait_recv()
+
+            wait_recv(y_copies(t + 4), has_right, has_left)
+        four(12)
+        if onward_x:
+
+            @pl.when(has_up)
+            def _():
+                onward_x[1].start()
+
+        four(8)
+        if onward_x:
+            start(y_copies(t + 5), has_left, has_right)
 
     wait_recv(x_copies(0), has_up, has_down)
     wait_recv(x_copies(4), has_up, has_down)
@@ -407,31 +442,41 @@
             device_id=(d, b), device_id_type=MESH,
         ).start()
 
-    def plastic_on(step, carry):
+    def plastic_on(step):
         g = lax.rem(step + s // 8, 4)
         plastic_group(g)
         for k in range(8):
             pass_plastic(8 * g + lax.rem(s + k, 8))
-        return carry
 
     plastic_group(s // 8)
     pltpu.make_async_copy(plastic_two.at[s], out_plastic.at[s], own_sem.at[0]).start()
     for k in range(1, 8):
         pass_plastic(8 * (s // 8) + lax.rem(s + k, 8))
-    lax.fori_loop(1, 4, plastic_on, 0)
-
-    for t in range(1, SWEEPS):
-        wait_recv(x_copies(t), has_up, has_down)
-        wait_recv(y_copies(t), has_right, has_left)
-        sweep(t)
-
-    def prepare(x, most):
-        fields = [state[SWEEPS, f, x + 1] for f in range(4)]
-        squared = fields[0] * fields[0]
-        stiff[x + 1] = cond[x + 1] * (1.0 + 0.5 * squared / (1.0 + squared)) / (1.0 + plastic[x]) * factor
-        return tuple(jnp.maximum(most[f], jnp.abs(fields[f])) for f in range(4))
-
-    most = lax.fori_loop(0, EDGE, prepare, (zero_plane,) * 4)
+
+    sweep(1)
+    plastic_on(1)
+    sweep(2)
+    plastic_on(2)
+    sweep(3)
+
+    def beside(plane):
+        parts = [plane[:, 0:128], plane[:, 128:256]]
+        return [jnp.concatenate([pltpu.roll(part, turn, 1) for part in parts], axis=1) for turn in (1, 127)]
+
+    def prepare(k, most):
+        most = list(most)
+        for j in range(4):
+            x = 4 * k + j
+            fields = [state[SWEEPS, f, x + 1] for f in range(4)]
+            squared = fields[0] * fields[0]
+            stiffness = cond[x + 1] * (1.0 + 0.5 * squared / (1.0 + squared)) / (1.0 + plastic[x]) * factor
+            stiff[x + 1] = stiffness
+            for f, plane in enumerate([stiffness] + fields):
+                turned[f, 0, x], turned[f, 1, x] = beside(plane)
+            most = [jnp.maximum(most[f], jnp.abs(fields[f])) for f in range(4)]
+        return tuple(most)
+
+    most = lax.fori_loop(0, EDGE // 4, prepare, (zero_plane,) * 4)
     exponents = []
     exponent_row = jnp.zeros((1, 128), I32)
     scales = []
@@ -450,9 +495,17 @@
         begun = [ones] + [tuple(state[SWEEPS, f, x + 2, rows, lanes] for rows in halves) for f in range(4)]
         totals = {1: list(done), 0: list(active), -1: begun}
         own = {dx: [stiff[x + 1 - dx, rows, lanes] for rows in halves] for dx in (-1, 0, 1)}
-        near = shifted_pairs(own[0], row8)
-        fields = [
-            shifted_pairs([state[SWEEPS, f, x + 1, rows, lanes] for rows in halves], row8) for f in range(4)
+        centres = [own[0]] + [[state[SWEEPS, f, x + 1, rows, lanes] for rows in halves] for f in range(4)]
+        near, *fields = [
+            shifted_pairs(
+                (
+                    [turned[f, 0, x, rows, lanes] for rows in halves],
+                    centres[f],
+                    [turned[f, 1, x, rows, lanes] for rows in halves],
+                ),
+                row8,
+            )
+            for f in range(5)
         ]
         for dz in (-1, 0, 1):
             for dy in (-1, 0, 1):
@@ -479,26 +532,37 @@
         for j, rows in enumerate(halves):
             inverse[place, rows, lanes] = scale[j]
         for f in range(4):
-            field = [done[f + 1][j] * scale[j] for j in range(2)]
-            for n, pair in enumerate(shifted_pairs(field, row8)):
-                for j, rows in enumerate(halves):
-                    values[f, n, place, rows, lanes] = pair[j]
+            for j, rows in enumerate(halves):
+                stepped[f, place, rows, lanes] = done[f + 1][j] * scale[j]
 
     for side in range(2):
 
-        def source(x, carry):
-            done, active, begun = built(x, *carry, side)
-
-            @pl.when(x > 0)
-            def _():
-                finish(x, done, side)
-
-            return active, begun
+        def source(k, carry):
+            for j in range(2):
+                done, *carry = built(2 * k + j, *carry, side)
+                finish(2 * k + j, done, side)
+            return tuple(carry)
 
         lanes = slice(128 * side, 128 * side + 128)
         start_at = (ones,) + tuple(tuple(state[SWEEPS, f, 1, rows, lanes] for rows in halves) for f in range(4))
-        last, _ = lax.fori_loop(0, EDGE, source, ((ones,) * 5, start_at))
+        last, _ = lax.fori_loop(0, EDGE // 2, source, ((ones,) * 5, start_at))
         finish(EDGE, last, side)
+
+    def spread(k, carry):
+        for j in range(2):
+            x = 2 * k + j
+            for f in range(4):
+                plane = stepped[f, x + 1]
+                minus, plus = beside(plane)
+                for side in range(2):
+                    lanes = slice(128 * side, 128 * side + 128)
+                    three = [[part[rows, lanes] for rows in halves] for part in (minus, plane, plus)]
+                    for n, pair in enumerate(shifted_pairs(three, row8)):
+                        for i, rows in enumerate(halves):
+                            values[f, n, x + 1, rows, lanes] = pair[i]
+        return carry
+
+    lax.fori_loop(0, EDGE // 2, spread, 0)
 
     def smoothed(x):
         totals = [state[SWEEPS, f, x + 1] for f in range(4)]
@@ -515,15 +579,18 @@
             device_id=(m, b), device_id_type=MESH,
         ).start()
 
-    def second_plane(x):
+    def encode_plane(x, slot):
         codes = []
         for f, field in enumerate(smoothed(x)):
             part = jnp.abs(field) * scales[f]
             part = jnp.minimum(part * lax.rsqrt(part + 1e-37), 1.0) * 32767.0
             codes.append((jnp.where(field < 0.0, -part, part) + 32768.5).astype(I32))
-        words = [(codes[0] << 16) | codes[1], (codes[2] << 16) | codes[3]]
+        coded[slot, 0] = (codes[0] << 16) | codes[1]
+        coded[slot, 1] = (codes[2] << 16) | codes[3]
+
+    def turn_plane(x, slot):
         tiles = [
-            words[w][8 * half : 8 * half + 8, 128 * side : 128 * side + 128]
+            coded[slot, w, 8 * half : 8 * half + 8, 128 * side : 128 * side + 128]
             for half in range(2)
             for w in range(2)
             for side in range(2)
@@ -536,16 +603,24 @@
             send_one[m, 32:33, :] = exponent_row
 
     def second(step, carry):
-        x = lax.rem(step + chip, EDGE)
-        second_plane(x)
+        x, later = lax.rem(step + chip, EDGE), lax.rem(step + 1 + chip, EDGE)
+        slot = lax.rem(step, 2)
+        turn_plane(x, slot)
+        encode_plane(later, 1 - slot)
         send_plane(2 * x)
         send_plane(2 * x + 1)
         return carry
 
-    second_plane(chip)
+    encode_plane(chip, 0)
+    turn_plane(chip, 0)
     send_plane(sibling)
     recv_one[s, 0:33, :] = send_one[s, 0:33, :]
-    lax.fori_loop(1, EDGE, second, 0)
+    encode_plane(lax.rem(chip + 1, EDGE), 1)
+    lax.fori_loop(1, EDGE - 1, second, 0)
+    turn_plane(lax.rem(chip + EDGE - 1, EDGE), 1)
+    send_plane(2 * lax.rem(chip + EDGE - 1, EDGE))
+    send_plane(2 * lax.rem(chip + EDGE - 1, EDGE) + 1)
+    plastic_on(3)
     wait_all(recv_one.at[pl.ds(0, N_SLAB - 1), pl.ds(0, 33)], one_recv)
 
     def unpack(g, carry):
@@ -560,12 +635,12 @@
     lax.fori_loop(0, 8, unpack, 0)
 
     def onward_group(g):
-        place = pl.ds(pl.multiple_of(128 * g, 128), 128)
+        place = pl.ds(pl.multiple_of(256 * g, 256), 256)
         rows = jnp.dot(one_hot[place, :], table[...], preferred_element_type=F32)
         for w in range(2):
             parts = [rows[:, 128 * (4 * w + n) : 128 * (4 * w + n) + 128] for n in range(4)]
             words = joined(parts[0], parts[1]) | (joined(parts[2], parts[3]) << 16)
-            send_two[pl.ds(8 * g, 8), 16 * w : 16 * w + 16, :] = words.reshape(8, P_DEV, 128)
+            send_two[pl.ds(16 * g, 16), 16 * w : 16 * w + 16, :] = words.reshape(16, P_DEV, 128)
 
     def pass_on(d):
         pltpu.make_async_remote_copy(
@@ -573,18 +648,13 @@
             device_id=(d, b), device_id_type=MESH,
         ).start()
 
-    def onward(step, carry):
-        g = lax.rem(step + s // 8, 4)
+    for step in range(2):
+        g = lax.bitwise_xor(step, s // 16)
         onward_group(g)
-        for k in range(8):
-            pass_on(8 * g + lax.rem(s + k, 8))
-        return carry
-
-    onward_group(s // 8)
-    pltpu.make_async_copy(send_two.at[s], out_words.at[s], own_sem.at[1]).start()
-    for k in range(1, 8):
-        pass_on(8 * (s // 8) + lax.rem(s + k, 8))
-    lax.fori_loop(1, 4, onward, 0)
+        if step == 0:
+            pltpu.make_async_copy(send_two.at[s], out_words.at[s], own_sem.at[1]).start()
+        for k in range(1 - step, 16):
+            pass_on(16 * g + lax.rem(s + k, 16))
 
     sources = jnp.concatenate(
         [jnp.broadcast_to(recv_one[k, 32:33, :].astype(F32), (P_DEV, 128)) for k in range(N_SLAB)], axis=0
@@ -594,7 +664,7 @@
 
     for kind in (0, 1, 2, 3, 4, 5):
         wait_send(x_copies(kind), has_down, has_up)
-    for kind in (0, 1, 2, 3, 4):
+    for kind in range(8):
         wait_send(y_copies(kind), has_left, has_right)
     wait_all(plastic_one.at[pl.ds(0, N_SLAB - 1), pl.ds(0, 9)], pl_one_send)
     wait_all(send_one.at[pl.ds(0, N_SLAB - 1), pl.ds(0, 33)], one_send)
@@ -620,9 +690,10 @@
             jax.ShapeDtypeStruct((N_SLAB, 8, 128), I32),
             jax.ShapeDtypeStruct((P_DEV, 128), F32),
         ),
-        in_specs=[anywhere, anywhere, anywhere, vmem, smem, smem, smem],
+        in_specs=[anywhere] * 4 + [smem] * 3,
         out_specs=(anywhere, anywhere, vmem),
         scratch_shapes=[
+            pltpu.VMEM((EDGE,) + plane, F32),
             pltpu.VMEM((SWEEPS + 1, 4, EDGE + 2) + plane, F32),
             pltpu.VMEM((SWEEPS, 2, 4) + plane, F32),
             pltpu.VMEM((SWEEPS, 2, 4) + plane, F32),
@@ -636,6 +707,9 @@
             pltpu.VMEM((EDGE,) + plane, F32),
             pltpu.VMEM((EDGE,) + plane, F32),
             pltpu.VMEM((EDGE + 2,) + plane, F32),
+            pltpu.VMEM((5, 2, EDGE) + plane, F32),
+            pltpu.VMEM((4, EDGE + 1) + plane, F32),
+            pltpu.VMEM((2, 2) + plane, I32),
             pltpu.VMEM((2, 9) + plane, F32),
             pltpu.VMEM((26, EDGE + 2) + plane, F32),
             pltpu.VMEM((EDGE + 1,) + plane, F32),
@@ -651,11 +725,11 @@
             pltpu.VMEM((ROWS, 256), BF16),
             pltpu.VMEM((64, 128), I32),
             pltpu.VMEM((64, 128), I32),
-            dma((3,)),
+            dma((4,)),
             dma((6, 2)),
             dma((6, 2)),
-            dma((5, 2)),
-            dma((5, 2)),
+            dma((8, 2)),
+            dma((8, 2)),
             dma(()),
             dma(()),
             dma(()),

time: 65.9 us -> 58.1 us (0.88)
  Pallas kernels: 65.1 us -> 57.2 us
    pallas_call x1, Pallas kernels: 62.1 us -> 54.2 us  [move(): pl.pallas_call(move_kernel, name='sweep_solve_move', out_shape=(jax.Shape...]
where the time goes in v3:
time: 58.1 us; the launch traced here: 57.9 us
  Pallas kernels  57.2 us (98%)
  between operations  0.64 us (1%)
    pallas_call x1, Pallas kernels, move(): pl.pallas_call(move_kernel, name='sweep_solve_move', out_shape=(jax.Shape...  54.2 us
    pallas_call x1, Pallas kernels, decode(): pl.pallas_call(decode_kernel, name='decode', out_shape=(jax.ShapeDtypeStr...  2.99 us

profile of v3, /device:TPU:1, one launch (start us, length us, event | category | flops | bytes accessed | tf_op | source)
XLA Modules:
  0.0 57.9 jit_solution(449277341912072530)
XLA Ops:
  0.6 54.2 %sweep_solve_move.1 = (s32[32,32,128]{2,1,0:T(8,128)}, s32[32,8,128]{2,1,0:T(8,128)}, f32[16,128]{1,0:T(8,128)}) custom-call(f32[16,16,256]{2,1,0:T(8,128)} %thermal.1, f32[3,16,16,256]{3,2,1,0:T(8,128)} %deform.1, f32[16,16,256]{2,1,0:T(8,128)} %modulus.1, f32[16,16,256]{2,1,0:T(8,128)} %plastic_in.1, s32[1,1,16]{2,1,0:T(1,128)} %flag.1, ...), custom_call_target="tpu_custom_call" | custom-call | tf_op jit(solution)/shard_map/sweep_solve_move/pallas_call | solution.py:685
  54.9 3.0 %decode.1 = (f32[1,1,16,4096]{3,2,1,0:T(8,128)}, f32[1,1,3,16,4096]{4,3,2,1,0:T(8,128)}, f32[1,1,16,4096]{3,2,1,0:T(8,128)}) custom-call(s32[32,32,128]{2,1,0:T(8,128)} %get-tuple-element.9.words_in, s32[32,8,128]{2,1,0:T(8,128)} %get-tuple-element.10.plastic_in, f32[16,128]{1,0:T(8,128)} %get-tuple-element.11.exponents), custom_call_target="tpu_custom_call" | custom-call | tf_op jit(solution)/shard_map/decode/pallas_call | solution.py:803

commit v4 on v3

--- a/solution.py
+++ b/solution.py
@@ -80,14 +80,14 @@
 
 def move_kernel(
     thermal, deform, modulus, plastic_in, flag, holder, position,
-    out_words, out_plastic, out_exponents,
+    out_words, out_exponents,
     plastic, state, halo_y, stage_y, cond, cond_y, cond_stage,
     face_x, face_ym, face_yp, face_zm, face_zp, centre,
     stiff, turned, stepped, coded, weights, tile, inverse, values,
-    send_one, recv_one, send_two, plastic_one, plastic_got, plastic_two,
-    one_hot, table, plastic_table, swap_a, swap_b,
+    send_one, recv_one, send_two, plastic_one, plastic_got,
+    one_hot, table, plastic_table, swap_a, swap_b, exponents_here,
     load_sem, x_send, x_recv, y_send, y_recv,
-    one_send, one_recv, two_send, two_recv, pl_one_send, pl_one_recv, pl_two_send, pl_two_recv, own_sem,
+    one_send, one_recv, two_send, two_recv, pl_one_send, pl_one_recv, own_sem, exponents_sem,
 ):
     s = lax.axis_index("slab")
     b = lax.axis_index("blk")
@@ -97,20 +97,6 @@
     has_up, has_down = s < N_SLAB - 1, s > 0
     has_right, has_left = b < N_BLK - 1, b > 0
 
-    barrier = pltpu.get_barrier_semaphore()
-
-    for step in range(1, N_SLAB):
-        peer = lax.rem(s + step, N_SLAB)
-        pl.semaphore_signal(barrier, inc=1, device_id=(peer, b), device_id_type=MESH)
-
-    @pl.when(has_right)
-    def _():
-        pl.semaphore_signal(barrier, inc=1, device_id=(s, right), device_id_type=MESH)
-
-    @pl.when(has_left)
-    def _():
-        pl.semaphore_signal(barrier, inc=1, device_id=(s, left), device_id_type=MESH)
-
     loads = [
         pltpu.make_async_copy(thermal, state.at[0, 0, pl.ds(1, EDGE)], load_sem.at[0]),
         pltpu.make_async_copy(deform, state.at[0, pl.ds(1, 3), pl.ds(1, EDGE)], load_sem.at[1]),
@@ -120,6 +106,20 @@
     for load in loads:
         load.start()
 
+    barrier = pltpu.get_barrier_semaphore()
+
+    for step in range(1, N_SLAB):
+        peer = lax.rem(s + step, N_SLAB)
+        pl.semaphore_signal(barrier, inc=1, device_id=(peer, b), device_id_type=MESH)
+
+    @pl.when(has_right)
+    def _():
+        pl.semaphore_signal(barrier, inc=1, device_id=(s, right), device_id_type=MESH)
+
+    @pl.when(has_left)
+    def _():
+        pl.semaphore_signal(barrier, inc=1, device_id=(s, left), device_id_type=MESH)
+
     zero_plane = jnp.zeros((EDGE, DEPTH), F32)
 
     for has, place, side in ((has_down, 0, 0), (has_up, EDGE + 1, 1)):
@@ -139,6 +139,69 @@
             for t in range(SWEEPS):
                 for f in range(4):
                     halo_y[t, side, f] = zero_plane
+
+    row8 = row_of((8, 128))
+    group8 = lane_of((8, 128)) // EDGE
+    row = row_of((EDGE, DEPTH))
+    lane = lane_of((EDGE, DEPTH))
+    inner = lane & (EDGE - 1)
+
+    for dy in (-1, 0, 1):
+        for dz in (-1, 0, 1):
+            inside = (row + dy >= 0) & (row + dy < EDGE) & (inner + dz >= 0) & (inner + dz < EDGE)
+            reach = abs(dy) + abs(dz)
+            weights[0, plane_number(dy, dz)] = jnp.where(inside, 0.5 * WEIGHTS[reach], 0.0)
+            weights[1, plane_number(dy, dz)] = jnp.where(inside, 0.5 * WEIGHTS[reach + 1], 0.0)
+    for n in range(9):
+        for f in range(4):
+            values[f, n, 0] = zero_plane
+            values[f, n, EDGE + 1] = zero_plane
+    for number, (dx, dy, dz) in enumerate(OFFSETS):
+        if dx != 0:
+            tile[number, 1 if dx < 0 else EDGE] = zero_plane
+
+    factor = jnp.ones((1, DEPTH), F32)
+    lane_row = lane_of((1, DEPTH)) // EDGE
+    for p in range(P_DEV):
+        factor = jnp.where(lane_row == p, 1.0 + 3.0 * flag[0, 0, p].astype(F32), factor)
+
+    for load in loads:
+        load.wait()
+
+    def stage_first(x, carry):
+        for side, y in ((0, 0), (1, EDGE - 1)):
+            cond_stage[side, pl.ds(x, 1), :] = cond[x + 1, y : y + 1, :]
+            for f in range(4):
+                stage_y[0, side, f, pl.ds(x, 1), :] = state[0, f, x + 1, y : y + 1, :]
+        return carry
+
+    lax.fori_loop(0, EDGE, stage_first, 0)
+    slot_lane = lane_of((1, 128))
+    slot_row = jnp.zeros((1, 128), I32)
+    for p in range(P_DEV):
+        code = holder[0, 0, p] * P_DEV + position[0, 0, p]
+        slot_row = jnp.where(slot_lane == lax.rem(s, 8) * P_DEV + p, code, slot_row)
+
+    def plastic_planes(planes):
+        tiles = []
+        for x in planes:
+            root = plastic[x]
+            root = root * lax.rsqrt(root)
+            codes = jnp.clip((root - PLASTIC_LOW) * PLASTIC_STEPS + 0.5, 0.0, 65535.0).astype(I32)
+            words = (codes[:, 0:128] << 16) | codes[:, 128:256]
+            tiles += [words[0:8], words[8:16]]
+        tiles = swap_rows_and_groups(tiles, group8, swap_a, swap_b)
+        for k in range(8):
+            m = 2 * planes[k // 2] + k % 2
+            plastic_one[m, 0:8, :] = tiles[k]
+            plastic_one[m, 8:9, :] = slot_row
+
+    def plastic_turn(k, carry):
+        plastic_planes([4 * k + j for j in range(4)])
+        return carry
+
+    lax.fori_loop(0, 4, plastic_turn, 0)
+    plastic_got[s, 0:9, :] = plastic_one[s, 0:9, :]
 
     neighbours = 31 + has_right.astype(I32) + has_left.astype(I32)
     pl.semaphore_wait(barrier, neighbours)
@@ -220,31 +283,8 @@
 
     for kind in (5, 0, 4):
         start(x_copies(kind), has_down, has_up)
-    for load in loads:
-        load.wait()
-
-    def stage_first(x, carry):
-        for side, y in ((0, 0), (1, EDGE - 1)):
-            cond_stage[side, pl.ds(x, 1), :] = cond[x + 1, y : y + 1, :]
-            for f in range(4):
-                stage_y[0, side, f, pl.ds(x, 1), :] = state[0, f, x + 1, y : y + 1, :]
-        return carry
-
-    lax.fori_loop(0, EDGE, stage_first, 0)
     start(y_copies(4), has_left, has_right)
     start(y_copies(0), has_left, has_right)
-
-    row8 = row_of((8, 128))
-    group8 = lane_of((8, 128)) // EDGE
-    row = row_of((EDGE, DEPTH))
-    lane = lane_of((EDGE, DEPTH))
-    inner = lane & (EDGE - 1)
-
-    slot_lane = lane_of((1, 128))
-    slot_row = jnp.zeros((1, 128), I32)
-    for p in range(P_DEV):
-        code = holder[0, 0, p] * P_DEV + position[0, 0, p]
-        slot_row = jnp.where(slot_lane == lax.rem(s, 8) * P_DEV + p, code, slot_row)
 
     sibling = lax.bitwise_xor(s, 1)
 
@@ -254,55 +294,16 @@
             device_id=(m, b), device_id_type=MESH,
         ).start()
 
-    def plastic_planes(planes):
-        tiles = []
-        for x in planes:
-            root = plastic[x]
-            root = root * lax.rsqrt(root)
-            codes = jnp.clip((root - PLASTIC_LOW) * PLASTIC_STEPS + 0.5, 0.0, 65535.0).astype(I32)
-            words = (codes[:, 0:128] << 16) | codes[:, 128:256]
-            tiles += [words[0:8], words[8:16]]
-        tiles = swap_rows_and_groups(tiles, group8, swap_a, swap_b)
-        for k in range(8):
-            m = 2 * planes[k // 2] + k % 2
-            plastic_one[m, 0:8, :] = tiles[k]
-            plastic_one[m, 8:9, :] = slot_row
-
-    def plastic_out(step, carry):
+    def plastic_out(step):
         planes = [lax.rem(chip + 4 * step + j, EDGE) for j in range(4)]
-        plastic_planes(planes)
-        for x in planes:
+        if step == 0:
+            send_plastic(sibling)
+        for x in planes[step == 0 :]:
             send_plastic(2 * x)
             send_plastic(2 * x + 1)
-        return carry
-
-    planes = [lax.rem(chip + j, EDGE) for j in range(4)]
-    plastic_planes(planes)
-    send_plastic(sibling)
-    plastic_got[s, 0:9, :] = plastic_one[s, 0:9, :]
-    for x in planes[1:]:
-        send_plastic(2 * x)
-        send_plastic(2 * x + 1)
-    lax.fori_loop(1, 4, plastic_out, 0)
-
-    for dy in (-1, 0, 1):
-        for dz in (-1, 0, 1):
-            inside = (row + dy >= 0) & (row + dy < EDGE) & (inner + dz >= 0) & (inner + dz < EDGE)
-            reach = abs(dy) + abs(dz)
-            weights[0, plane_number(dy, dz)] = jnp.where(inside, 0.5 * WEIGHTS[reach], 0.0)
-            weights[1, plane_number(dy, dz)] = jnp.where(inside, 0.5 * WEIGHTS[reach + 1], 0.0)
-    for n in range(9):
-        for f in range(4):
-            values[f, n, 0] = zero_plane
-            values[f, n, EDGE + 1] = zero_plane
-    for number, (dx, dy, dz) in enumerate(OFFSETS):
-        if dx != 0:
-            tile[number, 1 if dx < 0 else EDGE] = zero_plane
-
-    factor = jnp.ones((1, DEPTH), F32)
-    lane_row = lane_of((1, DEPTH)) // EDGE
-    for p in range(P_DEV):
-        factor = jnp.where(lane_row == p, 1.0 + 3.0 * flag[0, 0, p].astype(F32), factor)
+
+    plastic_out(0)
+    plastic_out(1)
 
     wait_recv(x_copies(5), has_up, has_down)
     wait_recv(y_copies(4), has_right, has_left)
@@ -412,6 +413,11 @@
     def wait_all(ref, semaphore):
         pltpu.make_async_copy(ref, ref, semaphore).wait()
 
+    plastic_out(2)
+    sweep(1)
+    plastic_out(3)
+    sweep(2)
+
     wait_all(plastic_got.at[pl.ds(0, N_SLAB - 1), pl.ds(0, 9)], pl_one_recv)
     slot_id = row_of((ROWS, 128))
     for g in range(4):
@@ -430,33 +436,14 @@
 
     lax.fori_loop(0, 8, plastic_unpack, 0)
 
-    def plastic_group(g):
+    def plastic_group(g, carry):
         place = pl.ds(pl.multiple_of(128 * g, 128), 128)
         rows = jnp.dot(one_hot[place, :], plastic_table[...], preferred_element_type=F32)
         codes = joined(rows[:, 0:128], rows[:, 128:256]).reshape(8, P_DEV, 128)
-        plastic_two[pl.ds(8 * g, 8)] = (codes[:, 0:8] << 16) | codes[:, 8:16]
-
-    def pass_plastic(d):
-        pltpu.make_async_remote_copy(
-            plastic_two.at[d], out_plastic.at[s], pl_two_send, pl_two_recv,
-            device_id=(d, b), device_id_type=MESH,
-        ).start()
-
-    def plastic_on(step):
-        g = lax.rem(step + s // 8, 4)
-        plastic_group(g)
-        for k in range(8):
-            pass_plastic(8 * g + lax.rem(s + k, 8))
-
-    plastic_group(s // 8)
-    pltpu.make_async_copy(plastic_two.at[s], out_plastic.at[s], own_sem.at[0]).start()
-    for k in range(1, 8):
-        pass_plastic(8 * (s // 8) + lax.rem(s + k, 8))
-
-    sweep(1)
-    plastic_on(1)
-    sweep(2)
-    plastic_on(2)
+        send_two[pl.ds(8 * g, 8), 32:40, :] = (codes[:, 0:8] << 16) | codes[:, 8:16]
+        return carry
+
+    lax.fori_loop(0, 4, plastic_group, 0)
     sweep(3)
 
     def beside(plane):
@@ -620,7 +607,6 @@
     turn_plane(lax.rem(chip + EDGE - 1, EDGE), 1)
     send_plane(2 * lax.rem(chip + EDGE - 1, EDGE))
     send_plane(2 * lax.rem(chip + EDGE - 1, EDGE) + 1)
-    plastic_on(3)
     wait_all(recv_one.at[pl.ds(0, N_SLAB - 1), pl.ds(0, 33)], one_recv)
 
     def unpack(g, carry):
@@ -648,19 +634,22 @@
             device_id=(d, b), device_id_type=MESH,
         ).start()
 
-    for step in range(2):
-        g = lax.bitwise_xor(step, s // 16)
-        onward_group(g)
-        if step == 0:
-            pltpu.make_async_copy(send_two.at[s], out_words.at[s], own_sem.at[1]).start()
-        for k in range(1 - step, 16):
-            pass_on(16 * g + lax.rem(s + k, 16))
+    onward_group(0)
+    onward_group(1)
+    pltpu.make_async_copy(send_two.at[s], out_words.at[s], own_sem).start()
+    pass_on(sibling)
+    for k in range(1, EDGE):
+        d = 2 * lax.rem(chip + k, EDGE)
+        pass_on(d)
+        pass_on(d + 1)
 
     sources = jnp.concatenate(
         [jnp.broadcast_to(recv_one[k, 32:33, :].astype(F32), (P_DEV, 128)) for k in range(N_SLAB)], axis=0
     ).astype(BF16)
     mine = one_hot[pl.ds(pl.multiple_of(s * P_DEV, P_DEV), P_DEV), :]
-    out_exponents[...] = jnp.dot(mine, sources, preferred_element_type=F32)
+    exponents_here[...] = jnp.dot(mine, sources, preferred_element_type=F32)
+    exponents_out = pltpu.make_async_copy(exponents_here, out_exponents, exponents_sem)
+    exponents_out.start()
 
     for kind in (0, 1, 2, 3, 4, 5):
         wait_send(x_copies(kind), has_down, has_up)
@@ -668,17 +657,14 @@
         wait_send(y_copies(kind), has_left, has_right)
     wait_all(plastic_one.at[pl.ds(0, N_SLAB - 1), pl.ds(0, 9)], pl_one_send)
     wait_all(send_one.at[pl.ds(0, N_SLAB - 1), pl.ds(0, 33)], one_send)
-    wait_all(plastic_two.at[pl.ds(0, N_SLAB - 1)], pl_two_send)
     wait_all(send_two.at[pl.ds(0, N_SLAB - 1)], two_send)
-    pltpu.make_async_copy(plastic_two.at[s], out_plastic.at[s], own_sem.at[0]).wait()
-    pltpu.make_async_copy(send_two.at[s], out_words.at[s], own_sem.at[1]).wait()
-    wait_all(out_plastic.at[pl.ds(0, N_SLAB - 1)], pl_two_recv)
+    pltpu.make_async_copy(send_two.at[s], out_words.at[s], own_sem).wait()
+    exponents_out.wait()
     wait_all(out_words.at[pl.ds(0, N_SLAB - 1)], two_recv)
 
 
 def move(thermal, deform, modulus, plastic, flag, holder, position):
     anywhere = pl.BlockSpec(memory_space=pl.ANY)
-    vmem = pl.BlockSpec(memory_space=pltpu.VMEM)
     smem = pl.BlockSpec(memory_space=pltpu.SMEM)
     plane = (EDGE, DEPTH)
     dma = pltpu.SemaphoreType.DMA
@@ -686,12 +672,11 @@
         move_kernel,
         name="sweep_solve_move",
         out_shape=(
-            jax.ShapeDtypeStruct((N_SLAB, 32, 128), I32),
-            jax.ShapeDtypeStruct((N_SLAB, 8, 128), I32),
+            jax.ShapeDtypeStruct((N_SLAB, 40, 128), I32),
             jax.ShapeDtypeStruct((P_DEV, 128), F32),
         ),
         in_specs=[anywhere] * 4 + [smem] * 3,
-        out_specs=(anywhere, anywhere, vmem),
+        out_specs=(anywhere, anywhere),
         scratch_shapes=[
             pltpu.VMEM((EDGE,) + plane, F32),
             pltpu.VMEM((SWEEPS + 1, 4, EDGE + 2) + plane, F32),
@@ -716,15 +701,15 @@
             pltpu.VMEM((4, 9, EDGE + 2) + plane, F32),
             pltpu.VMEM((N_SLAB, 40, 128), I32),
             pltpu.VMEM((N_SLAB, 40, 128), I32),
-            pltpu.VMEM((N_SLAB, 32, 128), I32),
+            pltpu.VMEM((N_SLAB, 40, 128), I32),
             pltpu.VMEM((N_SLAB, 16, 128), I32),
             pltpu.VMEM((N_SLAB, 16, 128), I32),
-            pltpu.VMEM((N_SLAB, 8, 128), I32),
             pltpu.VMEM((ROWS, ROWS), BF16),
             pltpu.VMEM((ROWS, 1024), BF16),
             pltpu.VMEM((ROWS, 256), BF16),
             pltpu.VMEM((64, 128), I32),
             pltpu.VMEM((64, 128), I32),
+            pltpu.VMEM((P_DEV, 128), F32),
             dma((4,)),
             dma((6, 2)),
             dma((6, 2)),
@@ -738,7 +723,6 @@
             dma(()),
             dma(()),
             dma(()),
-            dma((2,)),
         ],
         compiler_params=pltpu.CompilerParams(
             collective_id=0, has_side_effects=True, vmem_limit_bytes=56 * 1024 * 1024
@@ -747,16 +731,17 @@
 
 
 def decode_kernel(
-    words_in, plastic_in, exponents, heat_out, moved_out, plastic_out, words, strain, heat, moved, straight, got, put
+    words_in, exponents_in, heat_out, moved_out, plastic_out, words, exponents, heat, moved, straight, got, put
 ):
     pieces = N_SLAB // 4
     fetch = [
         pltpu.make_async_copy(words_in.at[pl.ds(pieces * k, pieces)], words.at[pl.ds(pieces * k, pieces)], got.at[k])
         for k in range(4)
     ]
-    fetch.append(pltpu.make_async_copy(plastic_in, strain, got.at[4]))
+    fetch.insert(0, pltpu.make_async_copy(exponents_in, exponents, got.at[4]))
     for copy in fetch:
         copy.start()
+    fetch.pop(0).wait()
     scales = [
         jnp.broadcast_to(jnp.exp2(exponents[:, f : f + 1]) * (1.0 / (32767.0 * 32767.0)), (P_DEV, 128))
         for f in range(4)
@@ -782,10 +767,8 @@
         writes.append(pltpu.make_async_copy(moved.at[:, :, at], moved_out.at[0, 0, :, :, at], put.at[3 * k + 1]))
         for copy in writes[-2:]:
             copy.start()
-        if k == 0:
-            fetch[4].wait()
         for m in range(pieces * k, pieces * k + pieces):
-            word = strain[m]
+            word = words[m, 32:40, :]
             for part in range(2):
                 code = lax.shift_right_logical(word, 16) if part == 0 else word & 65535
                 root = code.astype(F32) * (1.0 / PLASTIC_STEPS) + PLASTIC_LOW
@@ -796,8 +779,7 @@
         copy.wait()
 
 
-def decode(words, plastic, exponents):
-    vmem = pl.BlockSpec(memory_space=pltpu.VMEM)
+def decode(words, exponents):
     anywhere = pl.BlockSpec(memory_space=pl.ANY)
     length = EDGE**3
     heat, moved, strain = pl.pallas_call(
@@ -808,11 +790,11 @@
             jax.ShapeDtypeStruct((1, 1, 3, P_DEV, length), F32),
             jax.ShapeDtypeStruct((1, 1, P_DEV, length), F32),
         ),
-        in_specs=[anywhere, anywhere, vmem],
+        in_specs=[anywhere, anywhere],
         out_specs=(anywhere,) * 3,
         scratch_shapes=[
-            pltpu.VMEM((N_SLAB, 32, 128), I32),
-            pltpu.VMEM((N_SLAB, 8, 128), I32),
+            pltpu.VMEM((N_SLAB, 40, 128), I32),
+            pltpu.VMEM((P_DEV, 128), F32),
             pltpu.VMEM((P_DEV, length), F32),
             pltpu.VMEM((3, P_DEV, length), F32),
             pltpu.VMEM((P_DEV, length), F32),
@@ -820,7 +802,7 @@
             pltpu.SemaphoreType.DMA((12,)),
         ],
         compiler_params=pltpu.CompilerParams(vmem_limit_bytes=56 * 1024 * 1024),
-    )(words, plastic, exponents)
+    )(words, exponents)
     return heat, moved.transpose(0, 1, 3, 2, 4), strain
 
 

time: 58.1 us -> 56.5 us (0.972)
  Pallas kernels: 57.2 us -> 55.7 us
    pallas_call x1, Pallas kernels: 2.99 us -> 2.15 us  [decode(): pl.pallas_call(decode_kernel, name='decode', out_shape=(jax.ShapeDtypeStr...]
    pallas_call x1, Pallas kernels: 54.2 us -> 53.6 us  [move(): pl.pallas_call(move_kernel, name='sweep_solve_move', out_shape=(jax.Shape...]
where the time goes in v4:
time: 56.5 us; the launch traced here: 56.3 us
  Pallas kernels  55.7 us (99%)
  between operations  0.64 us (1%)
    pallas_call x1, Pallas kernels, move(): pl.pallas_call(move_kernel, name='sweep_solve_move', out_shape=(jax.Shape...  53.6 us
    pallas_call x1, Pallas kernels, decode(): pl.pallas_call(decode_kernel, name='decode', out_shape=(jax.ShapeDtypeStr...  2.15 us

profile of v4, /device:TPU:1, one launch (start us, length us, event | category | flops | bytes accessed | tf_op | source)
XLA Modules:
  0.0 56.3 jit_solution(15998898815842833353)
XLA Ops:
  0.6 53.6 %sweep_solve_move.1 = (s32[32,40,128]{2,1,0:T(8,128)}, f32[16,128]{1,0:T(8,128)}) custom-call(f32[16,16,256]{2,1,0:T(8,128)} %thermal.1, f32[3,16,16,256]{3,2,1,0:T(8,128)} %deform.1, f32[16,16,256]{2,1,0:T(8,128)} %modulus.1, f32[16,16,256]{2,1,0:T(8,128)} %plastic_in.1, s32[1,1,16]{2,1,0:T(1,128)} %flag.1, s32[1,1,16]{2,1,0:T(1,128)} %holder.1, ...), custom_call_target="tpu_custom_call" | custom-call | tf_op jit(solution)/shard_map/sweep_solve_move/pallas_call | solution.py:671
  54.2 2.1 %decode.1 = (f32[1,1,16,4096]{3,2,1,0:T(8,128)}, f32[1,1,3,16,4096]{4,3,2,1,0:T(8,128)}, f32[1,1,16,4096]{3,2,1,0:T(8,128)}) custom-call(s32[32,40,128]{2,1,0:T(8,128)} %get-tuple-element.8.words_in, f32[16,128]{1,0:T(8,128)} %get-tuple-element.9.exponents_in), custom_call_target="tpu_custom_call" | custom-call | tf_op jit(solution)/shard_map/decode/pallas_call | solution.py:785

commit v5 on v4

--- a/solution.py
+++ b/solution.py
@@ -80,14 +80,14 @@
 
 def move_kernel(
     thermal, deform, modulus, plastic_in, flag, holder, position,
-    out_words, out_exponents,
+    out_words, out_plastic, out_exponents,
     plastic, state, halo_y, stage_y, cond, cond_y, cond_stage,
     face_x, face_ym, face_yp, face_zm, face_zp, centre,
     stiff, turned, stepped, coded, weights, tile, inverse, values,
-    send_one, recv_one, send_two, plastic_one, plastic_got,
+    send_one, recv_one, send_two, plastic_one, plastic_got, plastic_two,
     one_hot, table, plastic_table, swap_a, swap_b, exponents_here,
     load_sem, x_send, x_recv, y_send, y_recv,
-    one_send, one_recv, two_send, two_recv, pl_one_send, pl_one_recv, own_sem, exponents_sem,
+    one_send, one_recv, two_send, two_recv, pl_one_send, pl_one_recv, pl_two_send, pl_two_recv, own_sem, own_plastic_sem, exponents_sem,
 ):
     s = lax.axis_index("slab")
     b = lax.axis_index("blk")
@@ -440,10 +440,24 @@
         place = pl.ds(pl.multiple_of(128 * g, 128), 128)
         rows = jnp.dot(one_hot[place, :], plastic_table[...], preferred_element_type=F32)
         codes = joined(rows[:, 0:128], rows[:, 128:256]).reshape(8, P_DEV, 128)
-        send_two[pl.ds(8 * g, 8), 32:40, :] = (codes[:, 0:8] << 16) | codes[:, 8:16]
+        plastic_two[pl.ds(8 * g, 8)] = (codes[:, 0:8] << 16) | codes[:, 8:16]
         return carry
 
     lax.fori_loop(0, 4, plastic_group, 0)
+
+    def pass_plastic(number):
+        d = 2 * lax.rem(chip + 1 + number // 2, EDGE) + lax.rem(number, 2)
+        start_plastic(d)
+
+    def start_plastic(d):
+        pltpu.make_async_remote_copy(
+            plastic_two.at[d], out_plastic.at[s], pl_two_send, pl_two_recv,
+            device_id=(d, b), device_id_type=MESH,
+        ).start()
+
+    own_plastic = pltpu.make_async_copy(plastic_two.at[s], out_plastic.at[s], own_plastic_sem)
+    own_plastic.start()
+    start_plastic(sibling)
     sweep(3)
 
     def beside(plane):
@@ -525,6 +539,11 @@
     for side in range(2):
 
         def source(k, carry):
+            if side == 0:
+                pass_plastic(2 * k)
+                pass_plastic(2 * k + 1)
+            else:
+                pass_plastic(16 + k)
             for j in range(2):
                 done, *carry = built(2 * k + j, *carry, side)
                 finish(2 * k + j, done, side)
@@ -535,9 +554,13 @@
         last, _ = lax.fori_loop(0, EDGE // 2, source, ((ones,) * 5, start_at))
         finish(EDGE, last, side)
 
+    pass_plastic(28)
+    pass_plastic(29)
+
     def spread(k, carry):
-        for j in range(2):
-            x = 2 * k + j
+        pass_plastic(24 + k)
+        for j in range(4):
+            x = 4 * k + j
             for f in range(4):
                 plane = stepped[f, x + 1]
                 minus, plus = beside(plane)
@@ -549,7 +572,7 @@
                             values[f, n, x + 1, rows, lanes] = pair[i]
         return carry
 
-    lax.fori_loop(0, EDGE // 2, spread, 0)
+    lax.fori_loop(0, EDGE // 4, spread, 0)
 
     def smoothed(x):
         totals = [state[SWEEPS, f, x + 1] for f in range(4)]
@@ -658,6 +681,9 @@
     wait_all(plastic_one.at[pl.ds(0, N_SLAB - 1), pl.ds(0, 9)], pl_one_send)
     wait_all(send_one.at[pl.ds(0, N_SLAB - 1), pl.ds(0, 33)], one_send)
     wait_all(send_two.at[pl.ds(0, N_SLAB - 1)], two_send)
+    wait_all(plastic_two.at[pl.ds(0, N_SLAB - 1)], pl_two_send)
+    own_plastic.wait()
+    wait_all(out_plastic.at[pl.ds(0, N_SLAB - 1)], pl_two_recv)
     pltpu.make_async_copy(send_two.at[s], out_words.at[s], own_sem).wait()
     exponents_out.wait()
     wait_all(out_words.at[pl.ds(0, N_SLAB - 1)], two_recv)
@@ -672,11 +698,12 @@
         move_kernel,
         name="sweep_solve_move",
         out_shape=(
-            jax.ShapeDtypeStruct((N_SLAB, 40, 128), I32),
+            jax.ShapeDtypeStruct((N_SLAB, 32, 128), I32),
+            jax.ShapeDtypeStruct((N_SLAB, 8, 128), I32),
             jax.ShapeDtypeStruct((P_DEV, 128), F32),
         ),
         in_specs=[anywhere] * 4 + [smem] * 3,
-        out_specs=(anywhere, anywhere),
+        out_specs=(anywhere,) * 3,
         scratch_shapes=[
             pltpu.VMEM((EDGE,) + plane, F32),
             pltpu.VMEM((SWEEPS + 1, 4, EDGE + 2) + plane, F32),
@@ -701,9 +728,10 @@
             pltpu.VMEM((4, 9, EDGE + 2) + plane, F32),
             pltpu.VMEM((N_SLAB, 40, 128), I32),
             pltpu.VMEM((N_SLAB, 40, 128), I32),
-            pltpu.VMEM((N_SLAB, 40, 128), I32),
+            pltpu.VMEM((N_SLAB, 32, 128), I32),
             pltpu.VMEM((N_SLAB, 16, 128), I32),
             pltpu.VMEM((N_SLAB, 16, 128), I32),
+            pltpu.VMEM((N_SLAB, 8, 128), I32),
             pltpu.VMEM((ROWS, ROWS), BF16),
             pltpu.VMEM((ROWS, 1024), BF16),
             pltpu.VMEM((ROWS, 256), BF16),
@@ -723,6 +751,9 @@
             dma(()),
             dma(()),
             dma(()),
+            dma(()),
+            dma(()),
+            dma(()),
         ],
         compiler_params=pltpu.CompilerParams(
             collective_id=0, has_side_effects=True, vmem_limit_bytes=56 * 1024 * 1024
@@ -731,13 +762,14 @@
 
 
 def decode_kernel(
-    words_in, exponents_in, heat_out, moved_out, plastic_out, words, exponents, heat, moved, straight, got, put
+    words_in, plastic_in, exponents_in, heat_out, moved_out, plastic_out, words, strain, exponents, heat, moved, straight, got, put
 ):
     pieces = N_SLAB // 4
     fetch = [
         pltpu.make_async_copy(words_in.at[pl.ds(pieces * k, pieces)], words.at[pl.ds(pieces * k, pieces)], got.at[k])
         for k in range(4)
     ]
+    fetch.append(pltpu.make_async_copy(plastic_in, strain, got.at[5]))
     fetch.insert(0, pltpu.make_async_copy(exponents_in, exponents, got.at[4]))
     for copy in fetch:
         copy.start()
@@ -767,8 +799,10 @@
         writes.append(pltpu.make_async_copy(moved.at[:, :, at], moved_out.at[0, 0, :, :, at], put.at[3 * k + 1]))
         for copy in writes[-2:]:
             copy.start()
+        if k == 0:
+            fetch[4].wait()
         for m in range(pieces * k, pieces * k + pieces):
-            word = words[m, 32:40, :]
+            word = strain[m]
             for part in range(2):
                 code = lax.shift_right_logical(word, 16) if part == 0 else word & 65535
                 root = code.astype(F32) * (1.0 / PLASTIC_STEPS) + PLASTIC_LOW
@@ -779,7 +813,7 @@
         copy.wait()
 
 
-def decode(words, exponents):
+def decode(words, plastic, exponents):
     anywhere = pl.BlockSpec(memory_space=pl.ANY)
     length = EDGE**3
     heat, moved, strain = pl.pallas_call(
@@ -790,19 +824,20 @@
             jax.ShapeDtypeStruct((1, 1, 3, P_DEV, length), F32),
             jax.ShapeDtypeStruct((1, 1, P_DEV, length), F32),
         ),
-        in_specs=[anywhere, anywhere],
+        in_specs=[anywhere] * 3,
         out_specs=(anywhere,) * 3,
         scratch_shapes=[
-            pltpu.VMEM((N_SLAB, 40, 128), I32),
+            pltpu.VMEM((N_SLAB, 32, 128), I32),
+            pltpu.VMEM((N_SLAB, 8, 128), I32),
             pltpu.VMEM((P_DEV, 128), F32),
             pltpu.VMEM((P_DEV, length), F32),
             pltpu.VMEM((3, P_DEV, length), F32),
             pltpu.VMEM((P_DEV, length), F32),
-            pltpu.SemaphoreType.DMA((5,)),
+            pltpu.SemaphoreType.DMA((6,)),
             pltpu.SemaphoreType.DMA((12,)),
         ],
         compiler_params=pltpu.CompilerParams(vmem_limit_bytes=56 * 1024 * 1024),
-    )(words, exponents)
+    )(words, plastic, exponents)
     return heat, moved.transpose(0, 1, 3, 2, 4), strain
 
 

time: 56.5 us -> 55.5 us (0.982)
  Pallas kernels: 55.7 us -> 54.7 us
    pallas_call x1, Pallas kernels: 53.6 us -> 52.4 us  [move(): pl.pallas_call(move_kernel, name='sweep_solve_move', out_shape=(jax.Shape...]
where the time goes in v5:
time: 55.5 us; the launch traced here: 55.4 us
  Pallas kernels  54.7 us (99%)
  between operations  0.64 us (1%)
    pallas_call x1, Pallas kernels, move(): pl.pallas_call(move_kernel, name='sweep_solve_move', out_shape=(jax.Shape...  52.4 us
    pallas_call x1, Pallas kernels, decode(): pl.pallas_call(decode_kernel, name='decode', out_shape=(jax.ShapeDtypeStr...  2.31 us

profile of v5, /device:TPU:1, one launch (start us, length us, event | category | flops | bytes accessed | tf_op | source)
XLA Modules:
  0.0 55.4 jit_solution(1862216349201658955)
XLA Ops:
  0.6 52.4 %sweep_solve_move.1 = (s32[32,32,128]{2,1,0:T(8,128)}, s32[32,8,128]{2,1,0:T(8,128)}, f32[16,128]{1,0:T(8,128)}) custom-call(f32[16,16,256]{2,1,0:T(8,128)} %thermal.1, f32[3,16,16,256]{3,2,1,0:T(8,128)} %deform.1, f32[16,16,256]{2,1,0:T(8,128)} %modulus.1, f32[16,16,256]{2,1,0:T(8,128)} %plastic_in.1, s32[1,1,16]{2,1,0:T(1,128)} %flag.1, ...), custom_call_target="tpu_custom_call" | custom-call | tf_op jit(solution)/shard_map/sweep_solve_move/pallas_call | solution.py:697
  53.0 2.3 %decode.1 = (f32[1,1,16,4096]{3,2,1,0:T(8,128)}, f32[1,1,3,16,4096]{4,3,2,1,0:T(8,128)}, f32[1,1,16,4096]{3,2,1,0:T(8,128)}) custom-call(s32[32,32,128]{2,1,0:T(8,128)} %get-tuple-element.9.words_in, s32[32,8,128]{2,1,0:T(8,128)} %get-tuple-element.10.plastic_in, f32[16,128]{1,0:T(8,128)} %get-tuple-element.11.exponents_in), custom_call_target="tpu_custom_call" | custom-call | tf_op jit(solution)/shard_map/decode/pallas_call | solution.py:819

commit v6 on v5

--- a/solution.py
+++ b/solution.py
@@ -146,25 +146,6 @@
     lane = lane_of((EDGE, DEPTH))
     inner = lane & (EDGE - 1)
 
-    for dy in (-1, 0, 1):
-        for dz in (-1, 0, 1):
-            inside = (row + dy >= 0) & (row + dy < EDGE) & (inner + dz >= 0) & (inner + dz < EDGE)
-            reach = abs(dy) + abs(dz)
-            weights[0, plane_number(dy, dz)] = jnp.where(inside, 0.5 * WEIGHTS[reach], 0.0)
-            weights[1, plane_number(dy, dz)] = jnp.where(inside, 0.5 * WEIGHTS[reach + 1], 0.0)
-    for n in range(9):
-        for f in range(4):
-            values[f, n, 0] = zero_plane
-            values[f, n, EDGE + 1] = zero_plane
-    for number, (dx, dy, dz) in enumerate(OFFSETS):
-        if dx != 0:
-            tile[number, 1 if dx < 0 else EDGE] = zero_plane
-
-    factor = jnp.ones((1, DEPTH), F32)
-    lane_row = lane_of((1, DEPTH)) // EDGE
-    for p in range(P_DEV):
-        factor = jnp.where(lane_row == p, 1.0 + 3.0 * flag[0, 0, p].astype(F32), factor)
-
     for load in loads:
         load.wait()
 
@@ -176,33 +157,6 @@
         return carry
 
     lax.fori_loop(0, EDGE, stage_first, 0)
-    slot_lane = lane_of((1, 128))
-    slot_row = jnp.zeros((1, 128), I32)
-    for p in range(P_DEV):
-        code = holder[0, 0, p] * P_DEV + position[0, 0, p]
-        slot_row = jnp.where(slot_lane == lax.rem(s, 8) * P_DEV + p, code, slot_row)
-
-    def plastic_planes(planes):
-        tiles = []
-        for x in planes:
-            root = plastic[x]
-            root = root * lax.rsqrt(root)
-            codes = jnp.clip((root - PLASTIC_LOW) * PLASTIC_STEPS + 0.5, 0.0, 65535.0).astype(I32)
-            words = (codes[:, 0:128] << 16) | codes[:, 128:256]
-            tiles += [words[0:8], words[8:16]]
-        tiles = swap_rows_and_groups(tiles, group8, swap_a, swap_b)
-        for k in range(8):
-            m = 2 * planes[k // 2] + k % 2
-            plastic_one[m, 0:8, :] = tiles[k]
-            plastic_one[m, 8:9, :] = slot_row
-
-    def plastic_turn(k, carry):
-        plastic_planes([4 * k + j for j in range(4)])
-        return carry
-
-    lax.fori_loop(0, 4, plastic_turn, 0)
-    plastic_got[s, 0:9, :] = plastic_one[s, 0:9, :]
-
     neighbours = 31 + has_right.astype(I32) + has_left.astype(I32)
     pl.semaphore_wait(barrier, neighbours)
 
@@ -286,6 +240,33 @@
     start(y_copies(4), has_left, has_right)
     start(y_copies(0), has_left, has_right)
 
+    slot_lane = lane_of((1, 128))
+    slot_row = jnp.zeros((1, 128), I32)
+    for p in range(P_DEV):
+        code = holder[0, 0, p] * P_DEV + position[0, 0, p]
+        slot_row = jnp.where(slot_lane == lax.rem(s, 8) * P_DEV + p, code, slot_row)
+
+    def plastic_planes(planes):
+        tiles = []
+        for x in planes:
+            root = plastic[x]
+            root = root * lax.rsqrt(root)
+            codes = jnp.clip((root - PLASTIC_LOW) * PLASTIC_STEPS + 0.5, 0.0, 65535.0).astype(I32)
+            words = (codes[:, 0:128] << 16) | codes[:, 128:256]
+            tiles += [words[0:8], words[8:16]]
+        tiles = swap_rows_and_groups(tiles, group8, swap_a, swap_b)
+        for k in range(8):
+            m = 2 * planes[k // 2] + k % 2
+            plastic_one[m, 0:8, :] = tiles[k]
+            plastic_one[m, 8:9, :] = slot_row
+
+    def plastic_turn(k, carry):
+        plastic_planes([4 * k + j for j in range(4)])
+        return carry
+
+    lax.fori_loop(0, 4, plastic_turn, 0)
+    plastic_got[s, 0:9, :] = plastic_one[s, 0:9, :]
+
     sibling = lax.bitwise_xor(s, 1)
 
     def send_plastic(m):
@@ -304,6 +285,25 @@
 
     plastic_out(0)
     plastic_out(1)
+
+    for dy in (-1, 0, 1):
+        for dz in (-1, 0, 1):
+            inside = (row + dy >= 0) & (row + dy < EDGE) & (inner + dz >= 0) & (inner + dz < EDGE)
+            reach = abs(dy) + abs(dz)
+            weights[0, plane_number(dy, dz)] = jnp.where(inside, 0.5 * WEIGHTS[reach], 0.0)
+            weights[1, plane_number(dy, dz)] = jnp.where(inside, 0.5 * WEIGHTS[reach + 1], 0.0)
+    for n in range(9):
+        for f in range(4):
+            values[f, n, 0] = zero_plane
+            values[f, n, EDGE + 1] = zero_plane
+    for number, (dx, dy, dz) in enumerate(OFFSETS):
+        if dx != 0:
+            tile[number, 1 if dx < 0 else EDGE] = zero_plane
+
+    factor = jnp.ones((1, DEPTH), F32)
+    lane_row = lane_of((1, DEPTH)) // EDGE
+    for p in range(P_DEV):
+        factor = jnp.where(lane_row == p, 1.0 + 3.0 * flag[0, 0, p].astype(F32), factor)
 
     wait_recv(x_copies(5), has_up, has_down)
     wait_recv(y_copies(4), has_right, has_left)
@@ -539,19 +539,16 @@
     for side in range(2):
 
         def source(k, carry):
-            if side == 0:
-                pass_plastic(2 * k)
-                pass_plastic(2 * k + 1)
-            else:
-                pass_plastic(16 + k)
-            for j in range(2):
-                done, *carry = built(2 * k + j, *carry, side)
-                finish(2 * k + j, done, side)
+            for j in range(4 if side == 0 else 2):
+                pass_plastic(4 * k + j if side == 0 else 16 + 2 * k + j)
+            for j in range(4):
+                done, *carry = built(4 * k + j, *carry, side)
+                finish(4 * k + j, done, side)
             return tuple(carry)
 
         lanes = slice(128 * side, 128 * side + 128)
         start_at = (ones,) + tuple(tuple(state[SWEEPS, f, 1, rows, lanes] for rows in halves) for f in range(4))
-        last, _ = lax.fori_loop(0, EDGE // 2, source, ((ones,) * 5, start_at))
+        last, _ = lax.fori_loop(0, EDGE // 4, source, ((ones,) * 5, start_at))
         finish(EDGE, last, side)
 
     pass_plastic(28)

time: 55.5 us -> 55.3 us (level)
  no operation moved by 1% of the time
where the time goes in v6:
time: 55.3 us; the launch traced here: 55.2 us
  Pallas kernels  54.5 us (99%)
  between operations  0.64 us (1%)
    pallas_call x1, Pallas kernels, move(): pl.pallas_call(move_kernel, name='sweep_solve_move', out_shape=(jax.Shape...  52.2 us
    pallas_call x1, Pallas kernels, decode(): pl.pallas_call(decode_kernel, name='decode', out_shape=(jax.ShapeDtypeStr...  2.31 us

profile of v6, /device:TPU:1, one launch (start us, length us, event | category | flops | bytes accessed | tf_op | source)
XLA Modules:
  0.0 55.2 jit_solution(16741170183596862137)
XLA Ops:
  0.6 52.2 %sweep_solve_move.1 = (s32[32,32,128]{2,1,0:T(8,128)}, s32[32,8,128]{2,1,0:T(8,128)}, f32[16,128]{1,0:T(8,128)}) custom-call(f32[16,16,256]{2,1,0:T(8,128)} %thermal.1, f32[3,16,16,256]{3,2,1,0:T(8,128)} %deform.1, f32[16,16,256]{2,1,0:T(8,128)} %modulus.1, f32[16,16,256]{2,1,0:T(8,128)} %plastic_in.1, s32[1,1,16]{2,1,0:T(1,128)} %flag.1, ...), custom_call_target="tpu_custom_call" | custom-call | tf_op jit(solution)/shard_map/sweep_solve_move/pallas_call | solution.py:694
  52.9 2.3 %decode.1 = (f32[1,1,16,4096]{3,2,1,0:T(8,128)}, f32[1,1,3,16,4096]{4,3,2,1,0:T(8,128)}, f32[1,1,16,4096]{3,2,1,0:T(8,128)}) custom-call(s32[32,32,128]{2,1,0:T(8,128)} %get-tuple-element.9.words_in, s32[32,8,128]{2,1,0:T(8,128)} %get-tuple-element.10.plastic_in, f32[16,128]{1,0:T(8,128)} %get-tuple-element.11.exponents_in), custom_call_target="tpu_custom_call" | custom-call | tf_op jit(solution)/shard_map/decode/pallas_call | solution.py:816

commit v7 on v6

--- a/solution.py
+++ b/solution.py
@@ -640,13 +640,11 @@
 
     lax.fori_loop(0, 8, unpack, 0)
 
-    def onward_group(g):
-        place = pl.ds(pl.multiple_of(256 * g, 256), 256)
-        rows = jnp.dot(one_hot[place, :], table[...], preferred_element_type=F32)
-        for w in range(2):
-            parts = [rows[:, 128 * (4 * w + n) : 128 * (4 * w + n) + 128] for n in range(4)]
-            words = joined(parts[0], parts[1]) | (joined(parts[2], parts[3]) << 16)
-            send_two[pl.ds(16 * g, 16), 16 * w : 16 * w + 16, :] = words.reshape(16, P_DEV, 128)
+    def onward_word(w):
+        rows = jnp.dot(one_hot[...], table[:, 512 * w : 512 * w + 512], preferred_element_type=F32)
+        parts = [rows[:, 128 * n : 128 * n + 128] for n in range(4)]
+        words = joined(parts[0], parts[1]) | (joined(parts[2], parts[3]) << 16)
+        send_two[:, 16 * w : 16 * w + 16, :] = words.reshape(N_SLAB, P_DEV, 128)
 
     def pass_on(d):
         pltpu.make_async_remote_copy(
@@ -654,8 +652,8 @@
             device_id=(d, b), device_id_type=MESH,
         ).start()
 
-    onward_group(0)
-    onward_group(1)
+    onward_word(0)
+    onward_word(1)
     pltpu.make_async_copy(send_two.at[s], out_words.at[s], own_sem).start()
     pass_on(sibling)
     for k in range(1, EDGE):

time: 55.3 us -> 55.3 us (level)
  no operation moved by 1% of the time
where the time goes in v7:
time: 55.3 us; the launch traced here: 55.2 us
  Pallas kernels  54.5 us (99%)
  between operations  0.64 us (1%)
    pallas_call x1, Pallas kernels, move(): pl.pallas_call(move_kernel, name='sweep_solve_move', out_shape=(jax.Shape...  52.2 us
    pallas_call x1, Pallas kernels, decode(): pl.pallas_call(decode_kernel, name='decode', out_shape=(jax.ShapeDtypeStr...  2.31 us

profile of v7, /device:TPU:1, one launch (start us, length us, event | category | flops | bytes accessed | tf_op | source)
XLA Modules:
  0.0 55.2 jit_solution(15683085242133821563)
XLA Ops:
  0.6 52.2 %sweep_solve_move.1 = (s32[32,32,128]{2,1,0:T(8,128)}, s32[32,8,128]{2,1,0:T(8,128)}, f32[16,128]{1,0:T(8,128)}) custom-call(f32[16,16,256]{2,1,0:T(8,128)} %thermal.1, f32[3,16,16,256]{3,2,1,0:T(8,128)} %deform.1, f32[16,16,256]{2,1,0:T(8,128)} %modulus.1, f32[16,16,256]{2,1,0:T(8,128)} %plastic_in.1, s32[1,1,16]{2,1,0:T(1,128)} %flag.1, ...), custom_call_target="tpu_custom_call" | custom-call | tf_op jit(solution)/shard_map/sweep_solve_move/pallas_call | solution.py:692
  52.9 2.3 %decode.1 = (f32[1,1,16,4096]{3,2,1,0:T(8,128)}, f32[1,1,3,16,4096]{4,3,2,1,0:T(8,128)}, f32[1,1,16,4096]{3,2,1,0:T(8,128)}) custom-call(s32[32,32,128]{2,1,0:T(8,128)} %get-tuple-element.9.words_in, s32[32,8,128]{2,1,0:T(8,128)} %get-tuple-element.10.plastic_in, f32[16,128]{1,0:T(8,128)} %get-tuple-element.11.exponents_in), custom_call_target="tpu_custom_call" | custom-call | tf_op jit(solution)/shard_map/decode/pallas_call | solution.py:814
